TPU v7x, 128 devices: a whole 4x4x4 slice. The times are simulated.
128 devices in a mesh: dp: 16 (over z, y_lo, core), mp: 8 (over x, y_hi).
Axes of the slice: x: 4, y: 4 (y_hi: 2, y_lo: 2; y = y_hi * 2 + y_lo), z: 4, core: 2. Of those that a mesh axis runs over, the one named last changes fastest.
Arguments:
- learn_hidden: bfloat16 [8192, 15360], P('dp', 'mp'), may hold values from -6 to 6
- out_cot: bfloat16 [8192, 4096], P('dp'), may hold values from -0.3125 to 0.3125
- master: float32 [15360, 4096], P(('mp', 'dp')), may hold values from -0.046875 to 0.046875
- moment_one: float32 [15360, 4096], P(('mp', 'dp')), may hold values from -4 to 4
- moment_two: float32 [15360, 4096], P(('mp', 'dp')), may hold values from 0.1 to 1
- queries: bfloat16 [4, 768, 4096], P(None, 'dp', 'mp'), may hold values from -100 to 100
- keys_cache: bfloat16 [768, 128, 1024], P('dp', None, 'mp'), may hold values from -5 to 5
- values_cache: bfloat16 [768, 128, 1024], P('dp', None, 'mp'), may hold values from -6 to 6
- keys_new: bfloat16 [4, 768, 1024], P(None, 'dp', 'mp'), may hold values from -6 to 6
- values_new: bfloat16 [4, 768, 1024], P(None, 'dp', 'mp'), may hold values from -6 to 6
- lengths: int32 [768], P('dp'), may hold values from 2 to 128
- residual: bfloat16 [4, 768, 4096], P(None, 'dp', 'mp'), may hold values from -50 to 50
- unit_acts: bfloat16 [4, 768, 8, 1920], P(None, 'dp', 'mp'), may hold values from -6 to 6
Outputs:
- mixed: bfloat16 [4, 768, 4096], P(None, 'dp', 'mp')
- master_next: float32 [15360, 4096], P(('mp', 'dp'))
- moment_one_next: float32 [15360, 4096], P(('mp', 'dp'))
- moment_two_next: float32 [15360, 4096], P(('mp', 'dp'))
All inputs are finite; a program needn't handle non-finite values.
Results may differ from a plain program's by a relative error of at most 0.0095.
Values may be sent and summed in bfloat16 or wider, within the bound.
A program may use at most 128 MiB of HBM per device.

v0:
```python
import jax
import jax.numpy as jnp
from jax import lax
from jax.sharding import PartitionSpec as P

HEADS = 32
KV_HEADS = 8
HEAD_DIM = 128


beta_one = 0.9
beta_two = 0.999
learn_rate = 0.01
decay_rate = 0.1
adam_eps = 1e-08
bias_steps = 10.0


def attend(queries, keys_cache, values_cache, keys_new, values_new, lengths):
    step_count, row_count, row_width = queries.shape
    cache_len = keys_cache.shape[1]
    kv_local = keys_cache.shape[2] // HEAD_DIM
    per_group = HEADS // KV_HEADS
    query_heads = queries.reshape(step_count, row_count, kv_local, per_group, HEAD_DIM)
    cache_keys = keys_cache.reshape(row_count, cache_len, kv_local, HEAD_DIM)
    cache_values = values_cache.reshape(row_count, cache_len, kv_local, HEAD_DIM)
    new_keys = keys_new.reshape(step_count, row_count, kv_local, HEAD_DIM)
    new_values = values_new.reshape(step_count, row_count, kv_local, HEAD_DIM)
    score_scale = HEAD_DIM ** (-0.5)
    cache_scores = (
        jnp.einsum("trkgd,rlkd->trkgl", query_heads, cache_keys, preferred_element_type=jnp.float32)
        * score_scale
    )
    new_scores = (
        jnp.einsum("trkgd,srkd->trkgs", query_heads, new_keys, preferred_element_type=jnp.float32)
        * score_scale
    )
    visible = jnp.arange(cache_len)[None, :] < lengths[:, None]
    causal = jnp.arange(step_count)[:, None] >= jnp.arange(step_count)[None, :]
    cache_scores = jnp.where(visible[None, :, None, None, :], cache_scores, -jnp.inf)
    new_scores = jnp.where(causal[:, None, None, None, :], new_scores, -jnp.inf)
    highest = jnp.maximum(jnp.max(cache_scores, axis=-1), jnp.max(new_scores, axis=-1))
    cache_exp = jnp.exp(cache_scores - highest[..., None])
    new_exp = jnp.exp(new_scores - highest[..., None])
    exp_total = jnp.sum(cache_exp, axis=-1) + jnp.sum(new_exp, axis=-1)
    cache_probs = (cache_exp / exp_total[..., None]).astype(jnp.bfloat16)
    new_probs = (new_exp / exp_total[..., None]).astype(jnp.bfloat16)
    mixed_heads = jnp.einsum(
        "trkgl,rlkd->trkgd", cache_probs, cache_values, preferred_element_type=jnp.float32
    )
    mixed_heads = mixed_heads + jnp.einsum(
        "trkgs,srkd->trkgd", new_probs, new_values, preferred_element_type=jnp.float32
    )
    return mixed_heads.reshape(step_count, row_count, row_width).astype(jnp.bfloat16)


def make_adder(acts_view, portion):
    return jnp.einsum("amc,cmd->ad", acts_view, portion, preferred_element_type=jnp.float32)


def local(
    learn_hidden,
    out_cot,
    master,
    moment_one,
    moment_two,
    queries,
    keys_cache,
    values_cache,
    keys_new,
    values_new,
    lengths,
    residual,
    unit_acts,
):
    contract = (((0,), (0,)), ((), ()))
    gradient_rows = lax.psum_scatter(
        lax.dot_general(learn_hidden, out_cot, contract, preferred_element_type=jnp.float32).astype(
            jnp.bfloat16
        ),
        "dp",
        scatter_dimension=0,
        tiled=True,
    ).astype(jnp.float32)
    moment_one_next = beta_one * moment_one + (1.0 - beta_one) * gradient_rows
    moment_two_next = beta_two * moment_two + (1.0 - beta_two) * gradient_rows * gradient_rows
    first_hat = moment_one_next / (1.0 - beta_one**bias_steps)
    second_hat = moment_two_next / (1.0 - beta_two**bias_steps)
    master_next = master - learn_rate * (
        first_hat / (jnp.sqrt(second_hat) + adam_eps) + decay_rate * master
    )
    fresh_rows = master_next.astype(jnp.bfloat16)
    attended = attend(queries, keys_cache, values_cache, keys_new, values_new, lengths)
    stream = (residual.astype(jnp.float32) + attended.astype(jnp.float32)).astype(jnp.bfloat16)
    step_count, row_count, share_width = stream.shape
    unit_local = unit_acts.shape[3]
    width = fresh_rows.shape[1]
    mp_count = lax.axis_size("mp")
    own_rows = fresh_rows.shape[0]
    spread = fresh_rows.reshape(own_rows // mp_count, mp_count, width)
    unit_pieces = lax.all_to_all(spread, "mp", split_axis=1, concat_axis=1, tiled=True)
    acts_view = unit_acts.reshape(step_count * row_count, mp_count, unit_local // mp_count)
    running = make_adder(acts_view, lax.all_gather(unit_pieces, "dp", axis=0, tiled=True))
    partials = running.reshape(step_count, row_count, width)
    summed = lax.psum_scatter(
        partials.astype(jnp.bfloat16), "mp", scatter_dimension=2, tiled=True
    ).astype(jnp.float32)
    mixed = (stream.astype(jnp.float32) + summed).astype(jnp.bfloat16)
    return (mixed, master_next, moment_one_next, moment_two_next)


def solution(mesh):
    placed = (
        P("dp", "mp"),
        P("dp", None),
        P(("mp", "dp"), None),
        P(("mp", "dp"), None),
        P(("mp", "dp"), None),
        P(None, "dp", "mp"),
        P("dp", None, "mp"),
        P("dp", None, "mp"),
        P(None, "dp", "mp"),
        P(None, "dp", "mp"),
        P("dp"),
        P(None, "dp", "mp"),
        P(None, "dp", "mp", None),
    )
    return jax.shard_map(
        local,
        mesh=mesh,
        in_specs=placed,
        out_specs=(
            P(None, "dp", "mp"),
            P(("mp", "dp"), None),
            P(("mp", "dp"), None),
            P(("mp", "dp"), None),
        ),
        check_vma=False,
    )
```

profile of v0, /device:TPU:0, one launch (start us, length us, event | category | flops | bytes accessed | tf_op | source)
XLA Modules:
  0.0 404.9 jit_solution(5125808301039905497)
XLA Ops:
  7.2 1.5 copy-done
  8.7 13.4 %convolution_convert_fusion = bf16[1920,4096]{1,0:T(8,128)(2,1)} fusion(bf16[512,1920]{1,0:T(8,128)(2,1)S(1)} %copy-done, bf16[512,4096]{1,0:T(8,128)(2,1)} %param.14), kind=kOutput, calls=%fused_computation | convolution fusion | flops 8060928000 | bytes 21889024 | tf_op jit(solution)/shard_map/dot_general | solution.py:78
  22.2 174.6 %reduce-scatter.3.cloned.1.call-done = bf16[120,4096]{1,0:T(8,128)(2,1)} async-done(((bf16[1920,4096]{1,0:T(8,128)(2,1)}), bf16[120,4096]{1,0:T(8,128)(2,1)}) %reduce-scatter.3.cloned.1.call-update) | async-done | bytes 983056 | tf_op jit(solution)/shard_map/reduce_scatter | solution.py:77
  196.7 6.6 %convert_bitcast_fusion = (bf16[15,8,4096]{2,1,0:T(8,128)(2,1)S(1)}, f32[120,4096]{1,0:T(8,128)}, f32[120,4096]{1,0:T(8,128)}, f32[120,4096]{1,0:T(8,128)}) fusion(f32[120,4096]{1,0:T(8,128)} %param.15, bf16[120,4096]{1,0:T(8,128)(2,1)} %reduce-scatter.3.cloned.1.call-done, f32[120,4096]{1,0:T(8,128)} %param.16, f32[120,4096]{1,0:T(8,128)} %param.17), kind=kLoop, calls=%fused_computation.23 | loop fusion | flops 8355840 | bytes 13762560 | tf_op jit(solution)/shard_map/reshape | solution.py:100
  203.4 0.5 copy.39
  203.9 21.2 %all_to_all.5 = bf16[15,8,4096]{2,0,1:T(8,128)(2,1)S(1)} all-to-all(bf16[15,8,4096]{2,0,1:T(8,128)(2,1)S(1)} %copy.39), channel_id=1, replica_groups=mesh['dp'=16,'mp'=8] {'mp'}, dimensions={1} | all-to-all | bytes 1966080 | tf_op jit(solution)/shard_map/all_to_all | solution.py:101
  225.1 1.6 copy.40
  226.7 0.2 reduce-scatter.5.cloned.1.call-start
  226.9 1.3 reshape.126
  228.3 2.0 copy.41
  230.3 80.7 %all-gather.2.cloned.1.call-done = bf16[240,8,4096]{2,1,0:T(8,128)(2,1)} async-done(((bf16[15,8,4096]{2,1,0:T(8,128)(2,1)}), bf16[240,8,4096]{2,1,0:T(8,128)(2,1)}) %all-gather.2.cloned.1.call-update) | async-done | bytes 15728656 | tf_op jit(solution)/shard_map/all_gather | solution.py:103
  311.0 10.3 %fusion = bf16[4096,192]{0,1:T(8,128)(2,1)} fusion(bf16[240,8,4096]{2,1,0:T(8,128)(2,1)} %all-gather.2.cloned.1.call-done, bf16[192,8,240]{0,1,2:T(8,128)(2,1)} %copy.41), kind=kOutput, calls=%fused_computation.2 | convolution fusion | flops 3020685312 | bytes 18038784 | tf_op jit(solution)/shard_map/amc,cmd->ad/dot_general | solution.py:58
  321.4 0.5 copy-done.4
  322.0 0.1 copy-done.6
  322.1 1.9 fusion.38
  324.0 2.6 fusion.37
  326.6 0.4 fusion.26
  327.0 0.6 fusion.25
  327.6 0.7 fusion.3
  328.3 0.1 copy-done.7
  328.4 0.4 fusion.16
  328.8 0.2 reshape.127
  329.1 67.6 %reduce-scatter.5.cloned.1.call-done = bf16[4,48,512]{2,1,0:T(8,128)(2,1)} async-done(((bf16[4,48,4096]{2,1,0:T(8,128)(2,1)}), bf16[4,48,512]{2,1,0:T(8,128)(2,1)}) %reduce-scatter.5.cloned.1.call-update) | async-done | bytes 196624 | tf_op jit(solution)/shard_map/reduce_scatter | solution.py:105
  396.7 1.7 add_convert_fusion
  (22 shorter events, 0.3 us)
Async XLA Ops:
  7.2 1.6 copy-start
  7.2 189.5 %reduce-scatter.3.cloned.1.call-start = ((), (), s32[]{:S(2)}) async-start(), calls=%async_computation.3 | async-start | bytes 16711680 | tf_op jit(solution)/shard_map/reduce_scatter | solution.py:77
  22.1 288.9 %all-gather.2.cloned.1.call-start = ((), (), s32[]{:S(2)}) async-start(), calls=%async_computation.4 | async-start | bytes 16711680 | tf_op jit(solution)/shard_map/all_gather | solution.py:103
  225.1 1.8 copy-start.1
  226.7 170.0 %reduce-scatter.5.cloned.1.call-start = ((), (), s32[]{:S(2)}) async-start(), calls=%async_computation.5 | async-start | bytes 1769472 | tf_op jit(solution)/shard_map/reduce_scatter | solution.py:105
  230.3 91.0 %copy-start.2 = (bf16[4,48,512]{2,1,0:T(8,128)(2,1)S(1)}, bf16[4,48,512]{2,1,0:T(8,128)(2,1)}, u32[]{:S(2)}) copy-start(bf16[4,48,512]{2,1,0:T(8,128)(2,1)} %param.18) | copy-start | bytes 589828
  321.3 0.7 copy-start.4
  321.3 0.8 copy-start.6
  324.0 3.6 copy-start.5
  327.6 0.8 copy-start.7
  328.4 68.3 %copy-start.3 = (bf16[4,48,512]{2,1,0:T(8,128)(2,1)S(1)}, bf16[4,48,512]{2,1,0:T(8,128)(2,1)}, u32[]{:S(2)}) copy-start(bf16[4,48,512]{2,1,0:T(8,128)(2,1)} %param.24) | copy-start | bytes 589828
Sparse Core Ops, SparseCore 0:
  22.2 174.4 reduce-scatter.2
  226.8 84.1 all-gather.1
  321.5 75.1 reduce-scatter.4
where the time goes:
time: 405 us
  waiting for transfers between devices  323 us (80%)
  matrix products  29.2 us (7%)
  blocking collectives  21.2 us (5%)
  between operations  13.9 us (3%)
  other arithmetic  9.48 us (2%)
  local copies, waits for them, and re-layouts  8.02 us (2%)
    reduce_scatter x1, waiting for transfers between devices, local(): lax.psum_scatter(lax.dot_general(learn_hidden, out_cot, contract, preferr...  175 us
    all_gather x1, waiting for transfers between devices, local(): lax.all_gather(unit_pieces, 'dp', axis=0, tiled=True)  80.7 us
    reduce_scatter x1, waiting for transfers between devices, local(): lax.psum_scatter(partials.astype(jnp.bfloat16), 'mp', scatter_dimension=2...  67.6 us
    all_to_all x1, blocking collectives, local(): lax.all_to_all(spread, 'mp', split_axis=1, concat_axis=1, tiled=True)  21.2 us
    dot_general x1, matrix products, local(): lax.dot_general(learn_hidden, out_cot, contract, preferred_element_type=j...  13.4 us
    dot_general x1, matrix products, make_adder(): jnp.einsum('amc,cmd->ad', acts_view, portion, preferred_element_type=jnp....  10.3 us
  transfers between devices with their start and end apart: 3, of which 3 were waited for; matrix products, arithmetic and copies ran while one was open for 3% of the time, Pallas kernels for 0%

commit v1 on v0

--- a/solution.py
+++ b/solution.py
@@ -1,7 +1,208 @@
+import functools
 import jax
 import jax.numpy as jnp
 from jax import lax
+from jax.experimental import pallas as pl
+from jax.experimental.pallas import tpu as pltpu
 from jax.sharding import PartitionSpec as P
+
+MESHID = pl.DeviceIdType.MESH
+bf16, f32 = jnp.bfloat16, jnp.float32
+NZ = 5
+NY = 3
+W = 256
+HW = W // 2
+
+
+def coords():
+    dp, mp = lax.axis_index("dp"), lax.axis_index("mp")
+    return dp // 4, (dp // 2) % 2, dp % 2, mp // 2, mp % 2
+
+
+def place(z, y_lo, core, x, y_hi):
+    return ((z * 2 + y_lo) * 2 + core, x * 2 + y_hi)
+
+
+def grad_kernel(ht, cot, out, hs, cs, zs1, zsb, zs2, zr1, zrb, zr2, zhold, zown, zys, zyr,
+                yys, yyr, ys1, ysb, ys2, yr1, yrb, yr2, yhold, yown, gbuf,
+                in_sem, send_sem, recv_sem):
+    z, y_lo, core, x, y_hi = coords()
+    sib = place(z, y_lo, 1 - core, x, y_hi)
+    up = place((z + 1) % 4, y_lo, core, x, y_hi)
+    down = place((z + 3) % 4, y_lo, core, x, y_hi)
+    across = place(z, 1 - y_lo, core, x, y_hi)
+
+    barrier = pltpu.get_barrier_semaphore()
+    for other in (sib, up, down, across):
+        pl.semaphore_signal(barrier, inc=1, device_id=other, device_id_type=MESHID)
+    pl.semaphore_wait(barrier, 4)
+
+    count = [0]
+    sends = []
+
+    def send(src, dst, device):
+        i = count[0]
+        count[0] += 1
+        copy = pltpu.make_async_remote_copy(
+            src_ref=src, dst_ref=dst, send_sem=send_sem.at[i], recv_sem=recv_sem.at[i],
+            device_id=device, device_id_type=MESHID)
+        copy.start()
+        sends.append(copy)
+        return copy
+
+    chunks = NZ + NY
+    order = [0, 5, 1, 6, 2, 7, 3, 4]
+    h_own = pltpu.make_async_copy(ht, hs.at[:, :, pl.ds(0, 512)], in_sem.at[chunks])
+    h_own.start()
+    h_sib = send(ht, hs.at[:, :, pl.ds(512, 512)], sib)
+    c_own, c_sib = {}, {}
+    for j in order:
+        mine = pl.ds(pl.multiple_of(core * 2048 + j * W, W), W)
+        theirs = pl.ds(pl.multiple_of((1 - core) * 2048 + j * W, W), W)
+        c_own[j] = pltpu.make_async_copy(cot.at[:, mine], cs.at[j, pl.ds(0, 512)], in_sem.at[j])
+        c_own[j].start()
+        c_sib[j] = send(cot.at[:, theirs], cs.at[j, pl.ds(512, 512)], sib)
+    h_own.wait()
+    h_sib.wait_recv()
+
+    def ready(j):
+        c_own[j].wait()
+        c_sib[j].wait_recv()
+
+    def rows480(zb, j):
+        lhs = hs[pl.ds(2 * zb, 2)].reshape(480, 1024)
+        return jnp.dot(lhs, cs[j], preferred_element_type=f32)
+
+    def rows240(zb, yb, j):
+        return jnp.dot(hs[2 * zb + yb], cs[j], preferred_element_type=f32)
+
+    zp, zm, zf = (z + 1) % 4, (z + 3) % 4, (z + 2) % 4
+    state = {}
+
+    def ring_start(key, term, s1, sb, r1, rb, hold, own):
+        p = term(zf)
+        s1[0] = p[:, :HW].astype(bf16)
+        s1[1] = p[:, HW:].astype(bf16)
+        st = {"r1": [send(s1.at[0], r1.at[0], up), send(s1.at[1], r1.at[1], down)]}
+        p = term(zp)
+        sb[0] = p[:, HW:].astype(bf16)
+        b0 = send(sb.at[0], rb.at[0], up)
+        hold[0] = p[:, :HW]
+        p = term(zm)
+        sb[1] = p[:, :HW].astype(bf16)
+        b1 = send(sb.at[1], rb.at[1], down)
+        hold[1] = p[:, HW:]
+        st["rb"] = [b0, b1]
+        own[...] = term(z)
+        state[key] = st
+
+    def ring_mid(key, s2, r1, r2, hold):
+        st = state[key]
+        st["r2"] = []
+        for d, device in ((0, up), (1, down)):
+            st["r1"][d].wait_recv()
+            s2[d] = (hold[d] + r1[d].astype(f32)).astype(bf16)
+            st["r2"].append(send(s2.at[d], r2.at[d], device))
+
+    def ring_end(key, rb, r2, own):
+        st = state[key]
+        st["rb"][1].wait_recv()
+        st["r2"][0].wait_recv()
+        left = own[:, :HW] + rb[1].astype(f32) + r2[0].astype(f32)
+        st["rb"][0].wait_recv()
+        st["r2"][1].wait_recv()
+        right = own[:, HW:] + rb[0].astype(f32) + r2[1].astype(f32)
+        return left, right
+
+    gsend = []
+
+    def finish(j, left, right):
+        gbuf[j, :, :, pl.ds(0, HW)] = left.reshape(2, 120, HW)
+        gbuf[j, :, :, pl.ds(HW, HW)] = right.reshape(2, 120, HW)
+        cols = pl.ds(pl.multiple_of(core * 2048 + j * W, W), W)
+        gsend.append(send(gbuf.at[j, 1 - core], out.at[:, cols], sib))
+        out[:, cols] = gbuf[j, core]
+
+    def zc(k):
+        ready(k)
+        ring_start(("z", k), lambda zb: rows480(zb, k), zs1.at[k], zsb.at[k], zr1.at[k], zrb.at[k], zhold.at[k], zown.at[k])
+
+    def zm_(k):
+        ring_mid(("z", k), zs2.at[k], zr1.at[k], zr2.at[k], zhold.at[k])
+
+    def ze(k):
+        left, right = ring_end(("z", k), zrb.at[k], zr2.at[k], zown.at[k])
+        zown[k, :, pl.ds(0, HW)] = left
+        zown[k, :, pl.ds(HW, HW)] = right
+        theirs = pl.ds(pl.multiple_of((1 - y_lo) * 240, 16), 240)
+        zys[k] = zown[k, theirs, :].astype(bf16)
+        state[("zy", k)] = send(zys.at[k], zyr.at[k], across)
+
+    def zf_(k):
+        state[("zy", k)].wait_recv()
+        mine = pl.ds(pl.multiple_of(y_lo * 240, 16), 240)
+        total = zown[k, mine, :] + zyr[k].astype(f32)
+        finish(k, total[:, :HW], total[:, HW:])
+
+    def yc(k):
+        j = NZ + k
+        ready(j)
+        def body(zb, carry):
+            yys[k, zb] = rows240(zb, 1 - y_lo, j).astype(bf16)
+            return carry
+        lax.fori_loop(0, 4, body, 0)
+        state[("yy", k)] = send(yys.at[k], yyr.at[k], across)
+
+    def ys(k):
+        j = NZ + k
+        state[("yy", k)].wait_recv()
+        ring_start(("y", k), lambda zb: rows240(zb, y_lo, j) + yyr[k, zb].astype(f32),
+                   ys1.at[k], ysb.at[k], yr1.at[k], yrb.at[k], yhold.at[k], yown.at[k])
+
+    def ym(k):
+        ring_mid(("y", k), ys2.at[k], yr1.at[k], yr2.at[k], yhold.at[k])
+
+    def ye(k):
+        left, right = ring_end(("y", k), yrb.at[k], yr2.at[k], yown.at[k])
+        finish(NZ + k, left, right)
+
+    zc(0); yc(0); zc(1); yc(1); zm_(0); yc(2); zc(2); zm_(1); ys(0); ze(0); zc(3); zm_(2); ze(1); ym(0); ys(1)
+    zc(4); zm_(3); ze(2); ym(1); ye(0); ys(2); zf_(0); zm_(4); ze(3); zf_(1); ym(2); ye(1); zf_(2); ze(4); zf_(3); ye(2); zf_(4)
+
+    for copy in gsend:
+        copy.wait_recv()
+    for copy in sends:
+        copy.wait_send()
+
+
+def grad_sum(learn_hidden, out_cot):
+    ht = learn_hidden.T.reshape(8, 240, 512)
+    ring = lambda n, r: [pltpu.VMEM((n, 2, r, HW), bf16)] * 6 + [pltpu.VMEM((n, 2, r, HW), f32), pltpu.VMEM((n, r, W), f32)]
+    copies = 1 + 8 + NZ * 8 + NY * 8
+    return pl.pallas_call(
+        grad_kernel,
+        out_shape=jax.ShapeDtypeStruct((120, 4096), f32),
+        in_specs=[pl.BlockSpec(memory_space=pl.ANY)] * 2,
+        out_specs=pl.BlockSpec(memory_space=pltpu.VMEM),
+        scratch_shapes=[
+            pltpu.VMEM((8, 240, 1024), bf16),
+            pltpu.VMEM((NZ + NY, 1024, W), bf16),
+            *ring(NZ, 480),
+            pltpu.VMEM((NZ, 240, W), bf16),
+            pltpu.VMEM((NZ, 240, W), bf16),
+            pltpu.VMEM((NY, 4, 240, W), bf16),
+            pltpu.VMEM((NY, 4, 240, W), bf16),
+            *ring(NY, 240),
+            pltpu.VMEM((NZ + NY, 2, 120, W), f32),
+            pltpu.SemaphoreType.DMA((NZ + NY + 1,)),
+            pltpu.SemaphoreType.DMA((copies,)),
+            pltpu.SemaphoreType.DMA((copies,)),
+        ],
+        compiler_params=pltpu.CompilerParams(collective_id=0, has_side_effects=True, vmem_limit_bytes=52 * 2**20),
+        cost_estimate=pl.CostEstimate(flops=8053063680, bytes_accessed=8 * 2**20, transcendentals=0),
+        name="gradient_sum",
+    )(ht, out_cot)
+
 
 HEADS = 32
 KV_HEADS = 8
@@ -73,15 +274,7 @@
     residual,
     unit_acts,
 ):
-    contract = (((0,), (0,)), ((), ()))
-    gradient_rows = lax.psum_scatter(
-        lax.dot_general(learn_hidden, out_cot, contract, preferred_element_type=jnp.float32).astype(
-            jnp.bfloat16
-        ),
-        "dp",
-        scatter_dimension=0,
-        tiled=True,
-    ).astype(jnp.float32)
+    gradient_rows = grad_sum(learn_hidden, out_cot)
     moment_one_next = beta_one * moment_one + (1.0 - beta_one) * gradient_rows
     moment_two_next = beta_two * moment_two + (1.0 - beta_two) * gradient_rows * gradient_rows
     first_hat = moment_one_next / (1.0 - beta_one**bias_steps)

time: 405 us -> 288 us (0.71)
  waiting for transfers between devices: 323 us -> 150 us
  Pallas kernels: 0 us -> 68.3 us
  matrix products: 29.2 us -> 14.1 us
    reduce_scatter x1 -> x0, waiting for transfers between devices: 175 us -> none  [local(): lax.psum_scatter(lax.dot_general(learn_hidden, out_cot, contract, preferr...]
    pallas_call x0 -> x1, Pallas kernels: none -> 68.3 us  [grad_sum(): pl.pallas_call(grad_kernel, out_shape=jax.ShapeDtypeStruct((120, 4096), f...]
    dot_general x1 -> x0, matrix products: 13.4 us -> none  [local(): lax.dot_general(learn_hidden, out_cot, contract, preferred_element_type=j...]
    transpose x0 -> x1, local copies, waits for them, and re-layouts: none -> 4.09 us  [grad_sum(): ht = learn_hidden.T.reshape(8, 240, 512)]
  transfers between devices with their start and end apart: 3 -> 2, of which waited for: 3 -> 2; matrix products, arithmetic and copies ran while one was open for 3% -> 3% of each run, Pallas kernels for 0% -> 0%
where the time goes in v1:
time: 288 us
  waiting for transfers between devices  150 us (52%)
  Pallas kernels  68.3 us (24%)
  blocking collectives  24.4 us (8%)
  between operations  14.2 us (5%)
  matrix products  14.1 us (5%)
  local copies, waits for them, and re-layouts  10 us (3%)
  other arithmetic  6.53 us (2%)
    all_gather x1, waiting for transfers between devices, local(): lax.all_gather(unit_pieces, 'dp', axis=0, tiled=True)  80.7 us
    reduce_scatter x1, waiting for transfers between devices, local(): lax.psum_scatter(partials.astype(jnp.bfloat16), 'mp', scatter_dimension=2...  69.1 us
    pallas_call x1, Pallas kernels, grad_sum(): pl.pallas_call(grad_kernel, out_shape=jax.ShapeDtypeStruct((120, 4096), f...  68.3 us
    all_to_all x1, blocking collectives, local(): lax.all_to_all(spread, 'mp', split_axis=1, concat_axis=1, tiled=True)  24.4 us
    dot_general x1, matrix products, make_adder(): jnp.einsum('amc,cmd->ad', acts_view, portion, preferred_element_type=jnp....  10.1 us
  transfers between devices with their start and end apart: 2, of which 2 were waited for; matrix products, arithmetic and copies ran while one was open for 3% of the time, Pallas kernels for 0%

profile of v1, /device:TPU:0, one launch (start us, length us, event | category | flops | bytes accessed | tf_op | source)
XLA Modules:
  0.0 287.8 jit_solution(4942328725730335172)
XLA Ops:
  7.2 4.1 %copy.41 = bf16[1920,512]{1,0:T(8,128)(2,1)} copy(bf16[1920,512]{0,1:T(8,128)(2,1)} %bitcast.67) | data formatting | bytes 3932160 | tf_op jit(solution)/shard_map/transpose | solution.py:179
  11.3 68.3 %gradient_sum.1 = f32[120,4096]{1,0:T(8,128)S(1)} custom-call(bf16[8,240,512]{2,1,0:T(8,128)(2,1)} %bitcast.68, bf16[512,4096]{1,0:T(8,128)(2,1)} %cot.1), custom_call_target="tpu_custom_call" | custom-call | flops 8053063680 | bytes 8388608 | tf_op jit(solution)/shard_map/gradient_sum/pallas_call | solution.py:182
  79.6 3.7 %convert_bitcast_fusion = (bf16[15,8,4096]{2,1,0:T(8,128)(2,1)S(1)}, f32[120,4096]{1,0:T(8,128)}, f32[120,4096]{1,0:T(8,128)}, f32[120,4096]{1,0:T(8,128)}) fusion(f32[120,4096]{1,0:T(8,128)S(1)} %copy-done.1, f32[120,4096]{1,0:T(8,128)S(1)} %gradient_sum.1, f32[120,4096]{1,0:T(8,128)S(1)} %copy-done.2, f32[120,4096]{1,0:T(8,128)S(1)} %copy-done.3), kind=kLoop, calls=%fused_computation.21 | loop fusion | flops 7864320 | bytes 14745600 | tf_op jit(solution)/shard_map/reshape | solution.py:293
  83.3 0.5 copy.42
  83.9 24.4 %all_to_all.5 = bf16[15,8,4096]{2,0,1:T(8,128)(2,1)S(1)} all-to-all(bf16[15,8,4096]{2,0,1:T(8,128)(2,1)S(1)} %copy.42), channel_id=1, replica_groups=mesh['dp'=16,'mp'=8] {'mp'}, dimensions={1} | all-to-all | bytes 1966080 | tf_op jit(solution)/shard_map/all_to_all | solution.py:294
  108.3 1.6 copy.43
  109.9 0.3 reduce-scatter.2.cloned.1.call-start
  110.2 1.3 reshape.130
  111.5 1.4 copy.44
  113.0 80.7 %all-gather.2.cloned.1.call-done = bf16[240,8,4096]{2,1,0:T(8,128)(2,1)} async-done(((bf16[15,8,4096]{2,1,0:T(8,128)(2,1)}), bf16[240,8,4096]{2,1,0:T(8,128)(2,1)}) %all-gather.2.cloned.1.call-update) | async-done | bytes 15728656 | tf_op jit(solution)/shard_map/all_gather | solution.py:296
  193.7 10.1 %fusion = bf16[4096,192]{0,1:T(8,128)(2,1)} fusion(bf16[240,8,4096]{2,1,0:T(8,128)(2,1)} %all-gather.2.cloned.1.call-done, bf16[192,8,240]{0,1,2:T(8,128)(2,1)S(1)} %copy.44), kind=kOutput, calls=%fused_computation.1 | convolution fusion | flops 3020685312 | bytes 18038784 | tf_op jit(solution)/shard_map/amc,cmd->ad/dot_general | solution.py:259
  203.9 0.5 copy-done.7
  204.5 0.1 iota_compare_fusion
  204.5 0.1 copy-done.9
  204.6 1.9 fusion.36
  206.5 1.0 fusion.35
  207.6 0.4 fusion.25
  208.0 0.6 fusion.24
  208.6 0.7 fusion.2
  209.3 0.1 copy-done.10
  209.4 0.4 fusion.15
  209.8 0.2 reshape.131
  210.0 69.1 %reduce-scatter.2.cloned.1.call-done = bf16[4,48,512]{2,1,0:T(8,128)(2,1)} async-done(((bf16[4,48,4096]{2,1,0:T(8,128)(2,1)}), bf16[4,48,512]{2,1,0:T(8,128)(2,1)}) %reduce-scatter.2.cloned.1.call-update) | async-done | bytes 196624 | tf_op jit(solution)/shard_map/reduce_scatter | solution.py:298
  279.2 1.7 add_convert_fusion
  (26 shorter events, 0.2 us)
Async XLA Ops:
  7.2 199.3 %copy-start = (bf16[48,128,128]{2,1,0:T(8,128)(2,1)S(1)}, bf16[48,128,128]{2,1,0:T(8,128)(2,1)}, u32[]{:S(2)}) copy-start(bf16[48,128,128]{2,1,0:T(8,128)(2,1)} %param.19) | copy-start | bytes 4718596
  7.2 186.5 %all-gather.2.cloned.1.call-start = ((), (), s32[]{:S(2)}) async-start(), calls=%async_computation.2 | async-start | bytes 16711680 | tf_op jit(solution)/shard_map/all_gather | solution.py:296
  11.3 68.3 %copy-start.1 = (f32[120,4096]{1,0:T(8,128)S(1)}, f32[120,4096]{1,0:T(8,128)}, u32[]{:S(2)}) copy-start(f32[120,4096]{1,0:T(8,128)} %param.15) | copy-start | bytes 5898244
  11.3 68.3 %copy-start.2 = (f32[120,4096]{1,0:T(8,128)S(1)}, f32[120,4096]{1,0:T(8,128)}, u32[]{:S(2)}) copy-start(f32[120,4096]{1,0:T(8,128)} %param.16) | copy-start | bytes 5898244
  11.3 68.3 %copy-start.3 = (f32[120,4096]{1,0:T(8,128)S(1)}, f32[120,4096]{1,0:T(8,128)}, u32[]{:S(2)}) copy-start(f32[120,4096]{1,0:T(8,128)} %param.17) | copy-start | bytes 5898244
  108.3 1.8 copy-start.4
  109.9 169.3 %reduce-scatter.2.cloned.1.call-start = ((), (), s32[]{:S(2)}) async-start(), calls=%async_computation.3 | async-start | bytes 1769472 | tf_op jit(solution)/shard_map/reduce_scatter | solution.py:298
  113.0 90.9 %copy-start.5 = (bf16[4,48,512]{2,1,0:T(8,128)(2,1)S(1)}, bf16[4,48,512]{2,1,0:T(8,128)(2,1)}, u32[]{:S(2)}) copy-start(bf16[4,48,512]{2,1,0:T(8,128)(2,1)} %param.18) | copy-start | bytes 589828
  203.8 0.7 copy-start.7
  203.8 0.8 copy-start.9
  206.5 2.1 copy-start.8
  208.6 0.8 copy-start.10
  209.4 69.8 %copy-start.6 = (bf16[4,48,512]{2,1,0:T(8,128)(2,1)S(1)}, bf16[4,48,512]{2,1,0:T(8,128)(2,1)}, u32[]{:S(2)}) copy-start(bf16[4,48,512]{2,1,0:T(8,128)(2,1)} %param.24) | copy-start | bytes 589828
Sparse Core Ops, SparseCore 0:
  110.0 83.6 all-gather.1
  203.9 75.1 reduce-scatter.1

commit v2 on v1

--- a/solution.py
+++ b/solution.py
@@ -255,8 +255,210 @@
     return mixed_heads.reshape(step_count, row_count, row_width).astype(jnp.bfloat16)
 
 
-def make_adder(acts_view, portion):
-    return jnp.einsum("amc,cmd->ad", acts_view, portion, preferred_element_type=jnp.float32)
+def project_kernel(fresh, acts, stream, out, wsend, wbuf, asend, abuf, part, r1, rb, s2, r2, q, u1, ub, v2, u2, fin,
+                   loc_sem, send_sem, recv_sem):
+    z, y_lo, core, x, y_hi = coords()
+    y, mp, slot = y_hi * 2 + y_lo, x * 2 + y_hi, z * 2 + core
+
+    def at_y(yy):
+        return place(z, yy % 2, core, x, yy // 2)
+
+    sib = place(z, y_lo, 1 - core, x, y_hi)
+    z_up, z_down = place((z + 1) % 4, y_lo, core, x, y_hi), place((z + 3) % 4, y_lo, core, x, y_hi)
+    x_up, x_down = place(z, y_lo, core, (x + 1) % 4, y_hi), place(z, y_lo, core, (x + 3) % 4, y_hi)
+    y_up, y_down = at_y((y + 1) % 4), at_y((y + 3) % 4)
+    across = place(z, 1 - y_lo, core, x, y_hi)
+    peers = []
+    for i in range(1, 8):
+        dx, dy = i // 2, i % 2
+        peers.append((((x + dx) % 4), ((y_hi + dy) % 2)))
+    peer_place = [place(z, y_lo, core, px, py) for px, py in peers]
+
+    barrier = pltpu.get_barrier_semaphore()
+    everyone = peer_place + [sib, z_up, z_down, y_up, y_down]
+    for other in everyone:
+        pl.semaphore_signal(barrier, inc=1, device_id=other, device_id_type=MESHID)
+    pl.semaphore_wait(barrier, len(everyone))
+
+    count = [0]
+    sends = []
+
+    def send(src, dst, device):
+        i = count[0]
+        count[0] += 1
+        copy = pltpu.make_async_remote_copy(
+            src_ref=src, dst_ref=dst, send_sem=send_sem.at[i], recv_sem=recv_sem.at[i],
+            device_id=device, device_id_type=MESHID)
+        copy.start()
+        sends.append(copy)
+        return copy
+
+    st = {}
+
+    row = lax.broadcasted_iota(jnp.int32, (128, 120), 0)
+    col = lax.broadcasted_iota(jnp.int32, (128, 120), 1)
+    pick = jnp.where(col == (row % 16) * 8 + row // 16, 1.0, 0.0).astype(bf16)
+    for b in range(8):
+        p = jnp.dot(pick, fresh[:, b * 512:(b + 1) * 512], preferred_element_type=f32).astype(bf16)
+        for k in range(4):
+            wsend[k, :, :, b * 128:(b + 1) * 128] = p[:, k * 128:(k + 1) * 128].reshape(8, 16, 128)
+
+    def spread(k):
+        st["a", k] = []
+        st["l", k] = pltpu.make_async_copy(wsend.at[k, mp], wbuf.at[k, mp, slot], loc_sem.at[k])
+        st["l", k].start()
+        for (px, py), device in zip(peers, peer_place):
+            st["a", k].append(send(wsend.at[k, px * 2 + py], wbuf.at[k, mp, slot], device))
+
+    spread(0)
+
+    unit = lax.broadcasted_iota(jnp.int32, (384, 256), 0)
+    lane = lax.broadcasted_iota(jnp.int32, (384, 256), 1)
+    own = (lane % 128) // 16
+    target = ((own // 2) * 4 + (lane // 128) * 2 + own % 2) * 15 + lane % 16
+    target = jnp.where(lane % 16 < 15, target, -1000)
+    for b in range(8):
+        start, shift = (b * 240) // 128 * 128, (b * 240) % 128
+        depth = 256 if shift + 240 <= 256 else 384
+        e = jnp.where(unit[:depth] - shift == target[:depth], 1.0, 0.0).astype(bf16)
+        a = jnp.dot(acts[:, start:start + depth], e, preferred_element_type=f32).astype(bf16)
+        asend[0, :, b * 128:(b + 1) * 128] = a[:, :128]
+        asend[1, :, b * 128:(b + 1) * 128] = a[:, 128:]
+    swap = send(asend.at[1 - y_lo], abuf.at[y_lo], across)
+    abuf[y_lo] = asend[y_lo]
+    for k in range(1, 4):
+        spread(k)
+
+    def gather_start(k):
+        st["l", k].wait()
+        for copy in st["a", k]:
+            copy.wait_recv()
+        mine = wbuf.at[k, :, slot]
+        st["u", k] = send(mine, wbuf.at[k, :, slot], z_up)
+        st["d", k] = send(mine, wbuf.at[k, :, slot], z_down)
+        st["s", k] = [send(mine, wbuf.at[k, :, slot], sib)]
+
+    def gather_mid(k):
+        below, above = ((z + 3) % 4) * 2 + core, ((z + 1) % 4) * 2 + core
+        st["u", k].wait_recv()
+        low = wbuf.at[k, pl.ds(0, 4), below]
+        st["ru", k] = send(low, wbuf.at[k, pl.ds(0, 4), below], z_up)
+        st["d", k].wait_recv()
+        high = wbuf.at[k, pl.ds(4, 4), above]
+        st["rd", k] = send(high, wbuf.at[k, pl.ds(4, 4), above], z_down)
+        st["s", k].append(send(wbuf.at[k, :, below], wbuf.at[k, :, below], sib))
+        st["s", k].append(send(wbuf.at[k, :, above], wbuf.at[k, :, above], sib))
+
+    def gather_end(k):
+        far = ((z + 2) % 4) * 2 + core
+        st["ru", k].wait_recv()
+        st["rd", k].wait_recv()
+        st["s", k].append(send(wbuf.at[k, :, far], wbuf.at[k, :, far], sib))
+
+    def multiply(k):
+        for copy in st["s", k]:
+            copy.wait_recv()
+        if k == 0:
+            swap.wait_recv()
+        lhs = abuf[...].reshape(384, 1024)
+
+        def body(n, carry):
+            cols = pl.ds(pl.multiple_of(n * 256, 256), 256)
+            rhs = wbuf[k, :, :, :, cols].reshape(1024, 256)
+            p = jnp.dot(lhs, rhs, preferred_element_type=f32).astype(bf16)
+            for i in range(4):
+                piece = p[(i % 2) * 192:(i % 2 + 1) * 192, (i // 2) * 128:(i // 2 + 1) * 128]
+                if k % 2 == 0:
+                    part[k, n, i] = piece
+                else:
+                    part[k, i, n] = piece
+            return carry
+
+        lax.fori_loop(0, 4, body, 0)
+        me, up, down = (x, x_up, x_down) if k % 2 == 0 else (y, y_up, y_down)
+        far, above, below = (me + 2) % 4, (me + 1) % 4, (me + 3) % 4
+        lo, hi = pl.ds(0, 2), pl.ds(2, 2)
+        st["r1", k] = [send(part.at[k, far, lo], r1.at[k, 0], up), send(part.at[k, far, hi], r1.at[k, 1], down)]
+        st["rb", k] = [send(part.at[k, above, hi], rb.at[k, 0], up), send(part.at[k, below, lo], rb.at[k, 1], down)]
+
+    def first_mid(k):
+        me, up, down = (x, x_up, x_down) if k % 2 == 0 else (y, y_up, y_down)
+        above, below = (me + 1) % 4, (me + 3) % 4
+        st["r1", k][0].wait_recv()
+        s2[k, 0] = (part[k, above, pl.ds(0, 2)].astype(f32) + r1[k, 0].astype(f32)).astype(bf16)
+        a = send(s2.at[k, 0], r2.at[k, 0], up)
+        st["r1", k][1].wait_recv()
+        s2[k, 1] = (part[k, below, pl.ds(2, 2)].astype(f32) + r1[k, 1].astype(f32)).astype(bf16)
+        st["r2", k] = [a, send(s2.at[k, 1], r2.at[k, 1], down)]
+
+    def first_end(k):
+        me = x if k % 2 == 0 else y
+        st["rb", k][1].wait_recv()
+        st["r2", k][0].wait_recv()
+        q[k, pl.ds(0, 2)] = (part[k, me, pl.ds(0, 2)].astype(f32) + rb[k, 1].astype(f32) + r2[k, 0].astype(f32)).astype(bf16)
+        st["rb", k][0].wait_recv()
+        st["r2", k][1].wait_recv()
+        q[k, pl.ds(2, 2)] = (part[k, me, pl.ds(2, 2)].astype(f32) + rb[k, 0].astype(f32) + r2[k, 1].astype(f32)).astype(bf16)
+        other, up, down = (y, y_up, y_down) if k % 2 == 0 else (x, x_up, x_down)
+        far, above, below = (other + 2) % 4, (other + 1) % 4, (other + 3) % 4
+        lo, hi = pl.ds(0, 96), pl.ds(96, 96)
+        st["u1", k] = [send(q.at[k, far, lo], u1.at[k, 0], up), send(q.at[k, far, hi], u1.at[k, 1], down)]
+        st["ub", k] = [send(q.at[k, above, hi], ub.at[k, 0], up), send(q.at[k, below, lo], ub.at[k, 1], down)]
+
+    def second_mid(k):
+        other, up, down = (y, y_up, y_down) if k % 2 == 0 else (x, x_up, x_down)
+        above, below = (other + 1) % 4, (other + 3) % 4
+        st["u1", k][0].wait_recv()
+        v2[k, 0] = (q[k, above, pl.ds(0, 96)].astype(f32) + u1[k, 0].astype(f32)).astype(bf16)
+        a = send(v2.at[k, 0], u2.at[k, 0], up)
+        st["u1", k][1].wait_recv()
+        v2[k, 1] = (q[k, below, pl.ds(96, 96)].astype(f32) + u1[k, 1].astype(f32)).astype(bf16)
+        st["u2", k] = [a, send(v2.at[k, 1], u2.at[k, 1], down)]
+
+    def second_end(k):
+        other = y if k % 2 == 0 else x
+        cols = pl.ds(k * 128, 128)
+        st["ub", k][1].wait_recv()
+        st["u2", k][0].wait_recv()
+        lo = q[k, other, pl.ds(0, 96)].astype(f32) + ub[k, 1].astype(f32) + u2[k, 0].astype(f32)
+        out[pl.ds(0, 96), cols] = (stream[pl.ds(0, 96), cols].astype(f32) + lo).astype(bf16)
+        st["ub", k][0].wait_recv()
+        st["u2", k][1].wait_recv()
+        hi = q[k, other, pl.ds(96, 96)].astype(f32) + ub[k, 0].astype(f32) + u2[k, 1].astype(f32)
+        out[pl.ds(96, 96), cols] = (stream[pl.ds(96, 96), cols].astype(f32) + hi).astype(bf16)
+
+    A, B, C, D, E, F, G, H = (gather_start, gather_mid, gather_end, multiply, first_mid, first_end, second_mid, second_end)
+    A(0); A(1); B(0); A(2); C(0); B(1); D(0); A(3); C(1); B(2); E(0); D(1); C(2); B(3); F(0); E(1); D(2); C(3)
+    G(0); F(1); E(2); D(3); H(0); G(1); F(2); E(3); H(1); G(2); F(3); H(2); G(3); H(3)
+    for copy in sends:
+        copy.wait_send()
+
+
+def project(fresh, acts, stream):
+    copies = 4 * 27 + 1
+    return pl.pallas_call(
+        project_kernel,
+        out_shape=jax.ShapeDtypeStruct((192, 512), bf16),
+        in_specs=[pl.BlockSpec(memory_space=pltpu.VMEM)] * 3,
+        out_specs=pl.BlockSpec(memory_space=pltpu.VMEM),
+        scratch_shapes=[
+            pltpu.VMEM((4, 8, 16, 1024), bf16),
+            pltpu.VMEM((4, 8, 8, 16, 1024), bf16),
+            pltpu.VMEM((2, 192, 1024), bf16),
+            pltpu.VMEM((2, 192, 1024), bf16),
+            pltpu.VMEM((4, 4, 4, 192, 128), bf16),
+            *[pltpu.VMEM((4, 2, 2, 192, 128), bf16)] * 4,
+            pltpu.VMEM((4, 4, 192, 128), bf16),
+            *[pltpu.VMEM((4, 2, 96, 128), bf16)] * 4,
+            pltpu.VMEM((8, 128), f32),
+            pltpu.SemaphoreType.DMA((4,)),
+            pltpu.SemaphoreType.DMA((copies,)),
+            pltpu.SemaphoreType.DMA((copies,)),
+        ],
+        compiler_params=pltpu.CompilerParams(collective_id=1, has_side_effects=True, vmem_limit_bytes=52 * 2**20),
+        cost_estimate=pl.CostEstimate(flops=3221225472, bytes_accessed=4 * 2**20, transcendentals=0),
+        name="project",
+    )(fresh, acts, stream)
 
 
 def local(
@@ -285,20 +487,7 @@
     fresh_rows = master_next.astype(jnp.bfloat16)
     attended = attend(queries, keys_cache, values_cache, keys_new, values_new, lengths)
     stream = (residual.astype(jnp.float32) + attended.astype(jnp.float32)).astype(jnp.bfloat16)
-    step_count, row_count, share_width = stream.shape
-    unit_local = unit_acts.shape[3]
-    width = fresh_rows.shape[1]
-    mp_count = lax.axis_size("mp")
-    own_rows = fresh_rows.shape[0]
-    spread = fresh_rows.reshape(own_rows // mp_count, mp_count, width)
-    unit_pieces = lax.all_to_all(spread, "mp", split_axis=1, concat_axis=1, tiled=True)
-    acts_view = unit_acts.reshape(step_count * row_count, mp_count, unit_local // mp_count)
-    running = make_adder(acts_view, lax.all_gather(unit_pieces, "dp", axis=0, tiled=True))
-    partials = running.reshape(step_count, row_count, width)
-    summed = lax.psum_scatter(
-        partials.astype(jnp.bfloat16), "mp", scatter_dimension=2, tiled=True
-    ).astype(jnp.float32)
-    mixed = (stream.astype(jnp.float32) + summed).astype(jnp.bfloat16)
+    mixed = project(fresh_rows, unit_acts.reshape(192, 1920), stream.reshape(192, 512)).reshape(stream.shape)
     return (mixed, master_next, moment_one_next, moment_two_next)
 
 

time: 288 us -> 169 us (0.59)
  waiting for transfers between devices: 150 us -> 0 us
  Pallas kernels: 68.3 us -> 150 us
  blocking collectives: 24.4 us -> 0 us
  between operations: 14.2 us -> 0.79 us
  matrix products: 14.1 us -> 3.98 us
  local copies, waits for them, and re-layouts: 10 us -> 6.31 us
    pallas_call x0 -> x1, Pallas kernels: none -> 82 us  [project(): pl.pallas_call(project_kernel, out_shape=jax.ShapeDtypeStruct((192, 512),...]
    all_gather x1 -> x0, waiting for transfers between devices: 80.7 us -> none  [local(): lax.all_gather(unit_pieces, 'dp', axis=0, tiled=True)]
    reduce_scatter x1 -> x0, waiting for transfers between devices: 69.1 us -> none  [local(): lax.psum_scatter(partials.astype(jnp.bfloat16), 'mp', scatter_dimension=2...]
    all_to_all x1 -> x0, blocking collectives: 24.4 us -> none  [local(): lax.all_to_all(spread, 'mp', split_axis=1, concat_axis=1, tiled=True)]
    dot_general x1 -> x0, matrix products: 10.1 us -> none  [make_adder(): jnp.einsum('amc,cmd->ad', acts_view, portion, preferred_element_type=jnp....]
    reshape x1 -> x0, other arithmetic: 3.69 us -> none  [local(): spread = fresh_rows.reshape(own_rows // mp_count, mp_count, width)]
    reshape x3 -> x0, local copies, waits for them, and re-layouts: 3.32 us -> none  [the longest x2 2.78 us: local(): unit_acts.reshape(step_count * row_count, mp_count, unit_local // mp_count)]
  transfers between devices with their start and end apart: 2 -> 0, of which waited for: 2 -> 0; matrix products, arithmetic and copies ran while one was open for 3% -> 0% of each run, Pallas kernels for 0% -> 0%
where the time goes in v2:
time: 169 us; the launch traced here: 167 us
  Pallas kernels  150 us (89%)
  local copies, waits for them, and re-layouts  6.31 us (4%)
  other arithmetic  5.94 us (4%)
  matrix products  3.98 us (2%)
    pallas_call x1, Pallas kernels, project(): pl.pallas_call(project_kernel, out_shape=jax.ShapeDtypeStruct((192, 512),...  82 us
    pallas_call x1, Pallas kernels, grad_sum(): pl.pallas_call(grad_kernel, out_shape=jax.ShapeDtypeStruct((120, 4096), f...  68.3 us
    transpose x1, local copies, waits for them, and re-layouts, grad_sum(): ht = learn_hidden.T.reshape(8, 240, 512)  3.98 us
    convert_element_type x1, other arithmetic, local(): fresh_rows = master_next.astype(jnp.bfloat16)  3.96 us

profile of v2, /device:TPU:0, one launch (start us, length us, event | category | flops | bytes accessed | tf_op | source)
XLA Modules:
  0.0 167.3 jit_solution(3769650506971676270)
XLA Ops:
  0.6 0.0 copy-start
  0.7 0.8 iota_compare_fusion
  1.5 1.0 reshape.128
  2.5 1.0 fusion.35
  3.6 0.0 copy-start.6
  3.6 0.0 copy-done.7
  3.6 1.9 %fusion.36 = (f32[4,48,4]{2,0,1:T(4,128)S(1)}, f32[4,48,1,4,4]{3,4,0,1,2:T(4,128)S(1)}) fusion(bf16[4,48,4,128]{3,2,1,0:T(4,128)(2,1)S(1)} %reshape.128, bf16[4,48,128,1]{2,1,0,3:T(8,128)(2,1)S(1)} %bitcast.60, pred[4,4]{1,0:T(4,128)(4,1)S(1)} %iota_compare_fusion.1), kind=kOutput, calls=%fused_computation.39 | convolution fusion | flops 794880 | bytes 261136 | tf_op jit(solution)/shard_map/trkgd,srkd->trkgs/dot_general | solution.py:236
  5.5 0.4 fusion.24
  5.8 0.6 fusion.23
  6.4 0.0 copy-done.6
  6.5 0.0 copy-start.8
  6.5 0.7 fusion.1
  7.2 0.1 copy-done.8
  7.3 0.4 fusion.14
  7.7 0.2 reshape.133
  7.9 0.3 copy-done.5
  8.2 0.1 fusion.22
  8.3 4.0 %copy.17 = bf16[1920,512]{1,0:T(8,128)(2,1)} copy(bf16[1920,512]{0,1:T(8,128)(2,1)} %bitcast.58) | data formatting | bytes 3932160 | tf_op jit(solution)/shard_map/transpose | solution.py:179
  12.3 68.3 %gradient_sum.1 = f32[120,4096]{1,0:T(8,128)S(1)} custom-call(bf16[8,240,512]{2,1,0:T(8,128)(2,1)} %bitcast.59, bf16[512,4096]{1,0:T(8,128)(2,1)} %cot.1), custom_call_target="tpu_custom_call" | custom-call | flops 8053063680 | bytes 8388608 | tf_op jit(solution)/shard_map/gradient_sum/pallas_call | solution.py:182
  80.6 0.0 copy-done.2
  80.6 0.0 copy-start.1
  80.6 4.0 %fusion.33 = (bf16[120,4096]{1,0:T(8,128)(2,1)}, f32[120,4096]{1,0:T(8,128)}, f32[120,4096]{1,0:T(8,128)}, f32[120,4096]{1,0:T(8,128)}) fusion(f32[120,4096]{1,0:T(8,128)S(1)} %copy-done.2, f32[120,4096]{1,0:T(8,128)S(1)} %gradient_sum.1, f32[120,4096]{1,0:T(8,128)S(1)} %copy-done.3, f32[120,4096]{1,0:T(8,128)S(1)} %copy-done.4), kind=kLoop, calls=%fused_computation.37 | loop fusion | flops 7864320 | bytes 14745600 | tf_op jit(solution)/shard_map/convert_element_type | solution.py:487
  84.6 82.0 %project.1 = bf16[192,512]{1,0:T(8,128)(2,1)S(1)} custom-call(bf16[120,4096]{1,0:T(8,128)(2,1)} %get-tuple-element.4.fresh, bf16[192,1920]{1,0:T(8,128)(2,1)S(1)} %bitcast.57, bf16[192,512]{1,0:T(8,128)(2,1)S(1)} %bitcast.56), custom_call_target="tpu_custom_call" | custom-call | flops 3221225472 | bytes 4194304 | tf_op jit(solution)/shard_map/project/pallas_call | solution.py:439
  166.6 0.7 copy.51
  (12 shorter events, 0.1 us)
Async XLA Ops:
  0.6 1.9 %copy-start = (bf16[48,128,128]{2,1,0:T(8,128)(2,1)S(1)}, bf16[48,128,128]{2,1,0:T(8,128)(2,1)}, u32[]{:S(2)}) copy-start(bf16[48,128,128]{2,1,0:T(8,128)(2,1)} %param.19) | copy-start | bytes 4718596
  0.6 2.9 %copy-start.7 = (bf16[4,48,128]{2,1,0:T(8,128)(2,1)S(1)}, bf16[4,48,128]{2,1,0:T(8,128)(2,1)}, u32[]{:S(2)}) copy-start(bf16[4,48,128]{2,1,0:T(8,128)(2,1)} %param.21) | copy-start | bytes 147460
  3.6 2.9 %copy-start.6 = (bf16[48,128,128]{2,1,0:T(8,128)(2,1)S(1)}, bf16[48,128,128]{2,1,0:T(8,128)(2,1)}, u32[]{:S(2)}) copy-start(bf16[48,128,128]{2,1,0:T(8,128)(2,1)} %param.20) | copy-start | bytes 4718596
  6.5 0.8 copy-start.8
  7.3 0.9 copy-start.5
  12.3 68.3 %copy-start.2 = (f32[120,4096]{1,0:T(8,128)S(1)}, f32[120,4096]{1,0:T(8,128)}, u32[]{:S(2)}) copy-start(f32[120,4096]{1,0:T(8,128)} %param.15) | copy-start | bytes 5898244
  12.3 68.3 %copy-start.3 = (f32[120,4096]{1,0:T(8,128)S(1)}, f32[120,4096]{1,0:T(8,128)}, u32[]{:S(2)}) copy-start(f32[120,4096]{1,0:T(8,128)} %param.16) | copy-start | bytes 5898244
  12.3 68.3 %copy-start.4 = (f32[120,4096]{1,0:T(8,128)S(1)}, f32[120,4096]{1,0:T(8,128)}, u32[]{:S(2)}) copy-start(f32[120,4096]{1,0:T(8,128)} %param.17) | copy-start | bytes 5898244
  80.6 4.0 %copy-start.1 = (bf16[4,48,1,1920]{3,1,2,0:T(8,128)(2,1)S(1)}, bf16[4,48,1,1920]{3,1,2,0:T(8,128)(2,1)}, u32[]{:S(2)}) copy-start(bf16[4,48,1,1920]{3,1,2,0:T(8,128)(2,1)} %param.25) | copy-start | bytes 2211844

commit v3 on v0

--- a/solution.py
+++ b/solution.py
@@ -1,19 +1,409 @@
+import functools
 import jax
 import jax.numpy as jnp
 from jax import lax
+from jax.experimental import pallas as pl
+from jax.experimental.pallas import tpu as pltpu
 from jax.sharding import PartitionSpec as P
 
+MESHID = pl.DeviceIdType.MESH
+bf16, f32 = jnp.bfloat16, jnp.float32
 HEADS = 32
 KV_HEADS = 8
 HEAD_DIM = 128
-
-
+CHUNKS = 4
+KIND = (("Z", "Y"), ("Z", "Y"), ("Z", "Y"), ("Z", "Y"))
+ORDER = [
+    ("yc", 1, 1), ("zc", 0, 0), ("zm", 0, 0), ("zc", 2, 0), ("yc", 0, 1), ("ze", 0, 0), ("zc", 1, 0), ("ys", 1, 1),
+    ("zm", 2, 0), ("zm", 1, 0), ("ym", 1, 1), ("yc", 2, 1), ("ys", 0, 1), ("zf", 0, 0), ("ym", 0, 1), ("ye", 1, 1),
+    ("zc", 3, 0), ("ye", 0, 1), ("ze", 1, 0), ("ad", 0), ("zm", 3, 0), ("ys", 2, 1), ("ze", 2, 0), ("zf", 1, 0),
+    ("ym", 2, 1), ("ad", 1), ("ga", 0), ("yc", 3, 1), ("ga", 1), ("ze", 3, 0), ("ye", 2, 1), ("zf", 2, 0), ("gb", 0),
+    ("ad", 2), ("gb", 1), ("gc", 0), ("ys", 3, 1), ("mm", 0), ("ym", 3, 1), ("zf", 3, 0), ("gc", 1), ("ga", 2),
+    ("ye", 3, 1), ("f2", 0), ("ad", 3), ("gb", 2), ("mm", 1), ("ga", 3), ("f3", 0), ("gc", 2), ("mm", 2), ("gb", 3),
+    ("f2", 2), ("gc", 3), ("f4", 0), ("f2", 1), ("mm", 3), ("f3", 1), ("f2", 3), ("f3", 2), ("f4", 1), ("f3", 3),
+    ("f4", 2), ("f5", 0), ("f4", 3), ("f5", 1), ("f5", 2), ("f5", 3),
+]
 beta_one = 0.9
 beta_two = 0.999
 learn_rate = 0.01
 decay_rate = 0.1
 adam_eps = 1e-08
 bias_steps = 10.0
+
+
+def coords():
+    dp, mp = lax.axis_index("dp"), lax.axis_index("mp")
+    return dp // 4, (dp // 2) % 2, dp % 2, mp // 2, mp % 2
+
+
+def place(z, y_lo, core, x, y_hi):
+    return ((z * 2 + y_lo) * 2 + core, x * 2 + y_hi)
+
+
+def fused_kernel(ht, cot, acts, stream, master, first, second, out, grad,
+                 hs, cs, zs1, zsb, zs2, zr1, zrb, zr2, zhold, zown, zys, zyr,
+                 yys, yyr, ys1, ysb, ys2, yr1, yrb, yr2, yhold, yown, gbuf, gall, adam,
+                 wsend, wbuf, asend, abuf, part, r1, rb, s2, r2, q, u1, ub, v2, u2,
+                 loc_sem, send_sem, recv_sem):
+    z, y_lo, core, x, y_hi = coords()
+    y, mp, slot = y_hi * 2 + y_lo, x * 2 + y_hi, z * 2 + core
+
+    def at_y(yy):
+        return place(z, yy % 2, core, x, yy // 2)
+
+    sib = place(z, y_lo, 1 - core, x, y_hi)
+    z_up, z_down = place((z + 1) % 4, y_lo, core, x, y_hi), place((z + 3) % 4, y_lo, core, x, y_hi)
+    x_up, x_down = place(z, y_lo, core, (x + 1) % 4, y_hi), place(z, y_lo, core, (x + 3) % 4, y_hi)
+    y_up, y_down = at_y((y + 1) % 4), at_y((y + 3) % 4)
+    across = place(z, 1 - y_lo, core, x, y_hi)
+    peers = [((x + i // 2) % 4, (y_hi + i % 2) % 2) for i in range(1, 8)]
+    peer_place = [place(z, y_lo, core, px, py) for px, py in peers]
+
+    barrier = pltpu.get_barrier_semaphore()
+    everyone = peer_place + [sib, z_up, z_down, y_up, y_down]
+    for other in everyone:
+        pl.semaphore_signal(barrier, inc=1, device_id=other, device_id_type=MESHID)
+    pl.semaphore_wait(barrier, len(everyone))
+
+    count = [0, 0]
+    sends = []
+    st = {}
+
+    def send(src, dst, device):
+        i = count[0]
+        count[0] += 1
+        copy = pltpu.make_async_remote_copy(
+            src_ref=src, dst_ref=dst, send_sem=send_sem.at[i], recv_sem=recv_sem.at[i],
+            device_id=device, device_id_type=MESHID)
+        copy.start()
+        sends.append(copy)
+        return copy
+
+    def local(src, dst):
+        i = count[1]
+        count[1] += 1
+        copy = pltpu.make_async_copy(src, dst, loc_sem.at[i])
+        copy.start()
+        return copy
+
+    h_own = local(ht, hs.at[:, :, pl.ds(0, 512)])
+    h_sib = send(ht, hs.at[:, :, pl.ds(512, 512)], sib)
+    for k in range(4):
+        for h in range(2):
+            st["c", k, h] = []
+            for i in range(2):
+                mine = pl.ds(pl.multiple_of((4 * core + 2 * h + i) * 512 + k * 128, 128), 128)
+                theirs = pl.ds(pl.multiple_of((4 - 4 * core + 2 * h + i) * 512 + k * 128, 128), 128)
+                lanes = pl.ds(i * 128, 128)
+                st["c", k, h].append(send(cot.at[:, theirs], cs.at[k, h, pl.ds(512, 512), lanes], sib))
+                st["c", k, h].append(local(cot.at[:, mine], cs.at[k, h, pl.ds(0, 512), lanes]))
+
+    def adam_fetch(k):
+        for b in range(8):
+            for i, ref in enumerate((master, first, second)):
+                st["m", k, b, i] = local(ref.at[:, pl.ds(b * 512 + k * 128, 128)], adam.at[k % 2, i, b])
+
+    adam_fetch(0)
+
+    unit = lax.broadcasted_iota(jnp.int32, (384, 256), 0)
+    lane = lax.broadcasted_iota(jnp.int32, (384, 256), 1)
+    owner = (lane % 128) // 16
+    target = ((owner // 2) * 4 + (lane // 128) * 2 + owner % 2) * 15 + lane % 16
+    target = jnp.where(lane % 16 < 15, target, -1000)
+    for b in range(8):
+        start, shift = (b * 240) // 128 * 128, (b * 240) % 128
+        depth = 256 if shift + 240 <= 256 else 384
+        e = jnp.where(unit[:depth] - shift == target[:depth], 1.0, 0.0).astype(bf16)
+        a = jnp.dot(acts[:, start:start + depth], e, preferred_element_type=f32).astype(bf16)
+        asend[0, :, b * 128:(b + 1) * 128] = a[:, :128]
+        asend[1, :, b * 128:(b + 1) * 128] = a[:, 128:]
+    swap = send(asend.at[1 - y_lo], abuf.at[y_lo], across)
+    abuf[y_lo] = asend[y_lo]
+
+    h_own.wait()
+    h_sib.wait_recv()
+
+    def ready(k, h):
+        for i in range(2):
+            st["c", k, h][2 * i].wait_recv()
+            st["c", k, h][2 * i + 1].wait()
+
+    zp, zm, zf = (z + 1) % 4, (z + 3) % 4, (z + 2) % 4
+
+    def ring_start(key, term, s1, sb, r1, rb, hold, own):
+        p = term(zf)
+        s1[0] = p[:, :128].astype(bf16)
+        s1[1] = p[:, 128:].astype(bf16)
+        st["r1", key] = [send(s1.at[0], r1.at[0], z_up), send(s1.at[1], r1.at[1], z_down)]
+        p = term(zp)
+        sb[0] = p[:, 128:].astype(bf16)
+        b0 = send(sb.at[0], rb.at[0], z_up)
+        hold[0] = p[:, :128].astype(hold.dtype)
+        p = term(zm)
+        sb[1] = p[:, :128].astype(bf16)
+        b1 = send(sb.at[1], rb.at[1], z_down)
+        hold[1] = p[:, 128:].astype(hold.dtype)
+        st["rb", key] = [b0, b1]
+        own[...] = term(z)
+
+    def ring_mid(key, s2, r1, r2, hold):
+        st["r2", key] = []
+        for d, device in ((0, z_up), (1, z_down)):
+            st["r1", key][d].wait_recv()
+            s2[d] = (hold[d].astype(f32) + r1[d].astype(f32)).astype(bf16)
+            st["r2", key].append(send(s2.at[d], r2.at[d], device))
+
+    def ring_end(key, rb, r2, own):
+        st["rb", key][1].wait_recv()
+        st["r2", key][0].wait_recv()
+        left = own[:, :128] + rb[1].astype(f32) + r2[0].astype(f32)
+        st["rb", key][0].wait_recv()
+        st["r2", key][1].wait_recv()
+        right = own[:, 128:] + rb[0].astype(f32) + r2[1].astype(f32)
+        return left, right
+
+    def finish(k, h, left, right):
+        gbuf[k, h, :, :, pl.ds(0, 128)] = left.reshape(2, 120, 128)
+        gbuf[k, h, :, :, pl.ds(128, 128)] = right.reshape(2, 120, 128)
+        st["g", k, h] = send(gbuf.at[k, h, 1 - core], gall.at[k, core, h], sib)
+        gall[k, core, h] = gbuf[k, h, core]
+
+    numbers = {"Z": 0, "Y": 0}
+    index = {}
+    for k in range(4):
+        for h in range(2):
+            index[k, h] = numbers[KIND[k][h]]
+            numbers[KIND[k][h]] += 1
+
+    def zc(k, h):
+        n = index[k, h]
+        ready(k, h)
+
+        def term(zb):
+            return jnp.dot(hs[pl.ds(2 * zb, 2)].reshape(480, 1024), cs[k, h], preferred_element_type=f32)
+
+        ring_start(("z", n), term, zs1.at[n], zsb.at[n], zr1.at[n], zrb.at[n], zhold.at[n], zown.at[n])
+
+    def zm_(k, h):
+        n = index[k, h]
+        ring_mid(("z", n), zs2.at[n], zr1.at[n], zr2.at[n], zhold.at[n])
+
+    def ze(k, h):
+        n = index[k, h]
+        left, right = ring_end(("z", n), zrb.at[n], zr2.at[n], zown.at[n])
+        zown[n, :, pl.ds(0, 128)] = left
+        zown[n, :, pl.ds(128, 128)] = right
+        theirs = pl.ds(pl.multiple_of((1 - y_lo) * 240, 16), 240)
+        zys[n] = zown[n, theirs, :].astype(bf16)
+        st["zy", n] = send(zys.at[n], zyr.at[n], across)
+
+    def zf_(k, h):
+        n = index[k, h]
+        st["zy", n].wait_recv()
+        mine = pl.ds(pl.multiple_of(y_lo * 240, 16), 240)
+        total = zown[n, mine, :] + zyr[n].astype(f32)
+        finish(k, h, total[:, :128], total[:, 128:])
+
+    def yc(k, h):
+        n = index[k, h]
+        ready(k, h)
+
+        def body(zb, carry):
+            yys[n, zb] = jnp.dot(hs[2 * zb + 1 - y_lo], cs[k, h], preferred_element_type=f32).astype(bf16)
+            return carry
+
+        lax.fori_loop(0, 4, body, 0)
+        st["yy", n] = send(yys.at[n], yyr.at[n], across)
+
+    def ys(k, h):
+        n = index[k, h]
+        st["yy", n].wait_recv()
+
+        def term(zb):
+            return jnp.dot(hs[2 * zb + y_lo], cs[k, h], preferred_element_type=f32) + yyr[n, zb].astype(f32)
+
+        ring_start(("y", n), term, ys1.at[n], ysb.at[n], yr1.at[n], yrb.at[n], yhold.at[n], yown.at[n])
+
+    def ym(k, h):
+        n = index[k, h]
+        ring_mid(("y", n), ys2.at[n], yr1.at[n], yr2.at[n], yhold.at[n])
+
+    def ye(k, h):
+        n = index[k, h]
+        left, right = ring_end(("y", n), yrb.at[n], yr2.at[n], yown.at[n])
+        finish(k, h, left, right)
+
+    def ad(k):
+        for h in range(2):
+            st["g", k, h].wait_recv()
+        if k < 3:
+            adam_fetch(k + 1)
+        row = lax.broadcasted_iota(jnp.int32, (128, 120), 0)
+        col = lax.broadcasted_iota(jnp.int32, (128, 120), 1)
+        pick = jnp.where(col == (row % 16) * 8 + row // 16, 1.0, 0.0).astype(bf16)
+        for b in range(8):
+            for i in range(3):
+                st["m", k, b, i].wait()
+            g = gall[k, b // 4, (b // 2) % 2, :, (b % 2) * 128:(b % 2 + 1) * 128]
+            st["o", k, b] = local(gall.at[k, b // 4, (b // 2) % 2, :, pl.ds((b % 2) * 128, 128)],
+                                  grad.at[:, pl.ds(b * 512 + k * 128, 128)])
+            m = adam[k % 2, 0, b]
+            one = beta_one * adam[k % 2, 1, b] + (1.0 - beta_one) * g
+            two = beta_two * adam[k % 2, 2, b] + (1.0 - beta_two) * g * g
+            one_hat = one / (1.0 - beta_one**bias_steps)
+            two_hat = two / (1.0 - beta_two**bias_steps)
+            new = m - learn_rate * (one_hat / (jnp.sqrt(two_hat) + adam_eps) + decay_rate * m)
+            p = jnp.dot(pick, new.astype(bf16), preferred_element_type=f32).astype(bf16)
+            wsend[k, :, :, b * 128:(b + 1) * 128] = p.reshape(8, 16, 128)
+        st["l", k] = local(wsend.at[k, mp], wbuf.at[k, mp, slot])
+        st["a", k] = []
+        for (px, py), device in zip(peers, peer_place):
+            st["a", k].append(send(wsend.at[k, px * 2 + py], wbuf.at[k, mp, slot], device))
+
+    def ga(k):
+        st["l", k].wait()
+        for copy in st["a", k]:
+            copy.wait_recv()
+        mine = wbuf.at[k, :, slot]
+        st["u", k] = send(mine, mine, z_up)
+        st["d", k] = send(mine, mine, z_down)
+        st["s", k] = [send(mine, mine, sib)]
+
+    def gb(k):
+        below, above = ((z + 3) % 4) * 2 + core, ((z + 1) % 4) * 2 + core
+        st["u", k].wait_recv()
+        low = wbuf.at[k, pl.ds(0, 4), below]
+        st["ru", k] = send(low, low, z_up)
+        st["d", k].wait_recv()
+        high = wbuf.at[k, pl.ds(4, 4), above]
+        st["rd", k] = send(high, high, z_down)
+        for s in (below, above):
+            st["s", k].append(send(wbuf.at[k, :, s], wbuf.at[k, :, s], sib))
+
+    def gc(k):
+        far = ((z + 2) % 4) * 2 + core
+        st["ru", k].wait_recv()
+        st["rd", k].wait_recv()
+        st["s", k].append(send(wbuf.at[k, :, far], wbuf.at[k, :, far], sib))
+
+    def mm(k):
+        for copy in st["s", k]:
+            copy.wait_recv()
+        if "swap" not in st:
+            swap.wait_recv()
+            st["swap"] = True
+        lhs = abuf[...].reshape(384, 1024)
+
+        def body(n, carry):
+            cols = pl.ds(pl.multiple_of(n * 256, 256), 256)
+            rhs = wbuf[k, :, :, :, cols].reshape(1024, 256)
+            p = jnp.dot(lhs, rhs, preferred_element_type=f32).astype(bf16)
+            for i in range(4):
+                part[k, n, i] = p[(i % 2) * 192:(i % 2 + 1) * 192, (i // 2) * 128:(i // 2 + 1) * 128]
+            return carry
+
+        lax.fori_loop(0, 4, body, 0)
+        far, above, below = (x + 2) % 4, (x + 1) % 4, (x + 3) % 4
+        lo, hi = pl.ds(0, 2), pl.ds(2, 2)
+        st["f1", k] = [send(part.at[k, far, lo], r1.at[k, 0], x_up), send(part.at[k, far, hi], r1.at[k, 1], x_down)]
+        st["fb", k] = [send(part.at[k, above, hi], rb.at[k, 0], x_up), send(part.at[k, below, lo], rb.at[k, 1], x_down)]
+
+    def f2(k):
+        above, below = (x + 1) % 4, (x + 3) % 4
+        st["f1", k][0].wait_recv()
+        s2[k, 0] = (part[k, above, pl.ds(0, 2)].astype(f32) + r1[k, 0].astype(f32)).astype(bf16)
+        a = send(s2.at[k, 0], r2.at[k, 0], x_up)
+        st["f1", k][1].wait_recv()
+        s2[k, 1] = (part[k, below, pl.ds(2, 2)].astype(f32) + r1[k, 1].astype(f32)).astype(bf16)
+        st["f2", k] = [a, send(s2.at[k, 1], r2.at[k, 1], x_down)]
+
+    def f3(k):
+        st["fb", k][1].wait_recv()
+        st["f2", k][0].wait_recv()
+        q[k, pl.ds(0, 2)] = (part[k, x, pl.ds(0, 2)].astype(f32) + rb[k, 1].astype(f32) + r2[k, 0].astype(f32)).astype(bf16)
+        st["fb", k][0].wait_recv()
+        st["f2", k][1].wait_recv()
+        q[k, pl.ds(2, 2)] = (part[k, x, pl.ds(2, 2)].astype(f32) + rb[k, 0].astype(f32) + r2[k, 1].astype(f32)).astype(bf16)
+        far, above, below = (y + 2) % 4, (y + 1) % 4, (y + 3) % 4
+        lo, hi = pl.ds(0, 96), pl.ds(96, 96)
+        st["g1", k] = [send(q.at[k, far, lo], u1.at[k, 0], y_up), send(q.at[k, far, hi], u1.at[k, 1], y_down)]
+        st["gb", k] = [send(q.at[k, above, hi], ub.at[k, 0], y_up), send(q.at[k, below, lo], ub.at[k, 1], y_down)]
+
+    def f4(k):
+        above, below = (y + 1) % 4, (y + 3) % 4
+        st["g1", k][0].wait_recv()
+        v2[k, 0] = (q[k, above, pl.ds(0, 96)].astype(f32) + u1[k, 0].astype(f32)).astype(bf16)
+        a = send(v2.at[k, 0], u2.at[k, 0], y_up)
+        st["g1", k][1].wait_recv()
+        v2[k, 1] = (q[k, below, pl.ds(96, 96)].astype(f32) + u1[k, 1].astype(f32)).astype(bf16)
+        st["g2", k] = [a, send(v2.at[k, 1], u2.at[k, 1], y_down)]
+
+    def f5(k):
+        cols = pl.ds(k * 128, 128)
+        st["gb", k][1].wait_recv()
+        st["g2", k][0].wait_recv()
+        lo = q[k, y, pl.ds(0, 96)].astype(f32) + ub[k, 1].astype(f32) + u2[k, 0].astype(f32)
+        out[pl.ds(0, 96), cols] = (stream[pl.ds(0, 96), cols].astype(f32) + lo).astype(bf16)
+        st["gb", k][0].wait_recv()
+        st["g2", k][1].wait_recv()
+        hi = q[k, y, pl.ds(96, 96)].astype(f32) + ub[k, 0].astype(f32) + u2[k, 1].astype(f32)
+        out[pl.ds(96, 96), cols] = (stream[pl.ds(96, 96), cols].astype(f32) + hi).astype(bf16)
+
+    steps = {"zc": zc, "zm": zm_, "ze": ze, "zf": zf_, "yc": yc, "ys": ys, "ym": ym, "ye": ye, "ad": ad,
+             "ga": ga, "gb": gb, "gc": gc, "mm": mm, "f2": f2, "f3": f3, "f4": f4, "f5": f5}
+    for name, *where in ORDER:
+        steps[name](*where)
+    for k in range(4):
+        for b in range(8):
+            st["o", k, b].wait()
+    for copy in sends:
+        copy.wait_send()
+
+
+def fused(learn_hidden, out_cot, acts, stream, master, first, second):
+    ht = learn_hidden.T.reshape(8, 240, 512)
+    kinds = [a for pair in KIND for a in pair]
+    nz, ny = max(kinds.count("Z"), 1), max(kinds.count("Y"), 1)
+
+    def ring(n, r):
+        return [pltpu.VMEM((n, 2, r, 128), bf16)] * 7 + [pltpu.VMEM((n, r, 256), f32)]
+
+    copies = 1 + 16 + 1 + 8 * 8 + 4 * 27
+    locals_ = 1 + 16 + 4 * (24 + 8 + 1)
+    return pl.pallas_call(
+        fused_kernel,
+        out_shape=(jax.ShapeDtypeStruct((192, 512), bf16), jax.ShapeDtypeStruct((120, 4096), f32)),
+        in_specs=[pl.BlockSpec(memory_space=pl.ANY)] * 2 + [pl.BlockSpec(memory_space=pltpu.VMEM)] * 2
+        + [pl.BlockSpec(memory_space=pl.ANY)] * 3,
+        out_specs=(pl.BlockSpec(memory_space=pltpu.VMEM), pl.BlockSpec(memory_space=pl.ANY)),
+        scratch_shapes=[
+            pltpu.VMEM((8, 240, 1024), bf16),
+            pltpu.VMEM((4, 2, 1024, 256), bf16),
+            *ring(nz, 480),
+            pltpu.VMEM((nz, 240, 256), bf16),
+            pltpu.VMEM((nz, 240, 256), bf16),
+            pltpu.VMEM((ny, 4, 240, 256), bf16),
+            pltpu.VMEM((ny, 4, 240, 256), bf16),
+            *ring(ny, 240),
+            pltpu.VMEM((4, 2, 2, 120, 256), f32),
+            pltpu.VMEM((4, 2, 2, 120, 256), f32),
+            pltpu.VMEM((2, 3, 8, 120, 128), f32),
+            pltpu.VMEM((4, 8, 16, 1024), bf16),
+            pltpu.VMEM((4, 8, 8, 16, 1024), bf16),
+            pltpu.VMEM((2, 192, 1024), bf16),
+            pltpu.VMEM((2, 192, 1024), bf16),
+            pltpu.VMEM((4, 4, 4, 192, 128), bf16),
+            *[pltpu.VMEM((4, 2, 2, 192, 128), bf16)] * 4,
+            pltpu.VMEM((4, 4, 192, 128), bf16),
+            *[pltpu.VMEM((4, 2, 96, 128), bf16)] * 4,
+            pltpu.SemaphoreType.DMA((locals_,)),
+            pltpu.SemaphoreType.DMA((copies,)),
+            pltpu.SemaphoreType.DMA((copies,)),
+        ],
+        compiler_params=pltpu.CompilerParams(collective_id=0, has_side_effects=True, vmem_limit_bytes=60 * 2**20),
+        cost_estimate=pl.CostEstimate(flops=11274289152, bytes_accessed=20 * 2**20, transcendentals=0),
+        name="fused",
+    )(ht, out_cot, acts, stream, master, first, second)
 
 
 def attend(queries, keys_cache, values_cache, keys_new, values_new, lengths):
@@ -52,10 +442,6 @@
         "trkgs,srkd->trkgd", new_probs, new_values, preferred_element_type=jnp.float32
     )
     return mixed_heads.reshape(step_count, row_count, row_width).astype(jnp.bfloat16)
-
-
-def make_adder(acts_view, portion):
-    return jnp.einsum("amc,cmd->ad", acts_view, portion, preferred_element_type=jnp.float32)
 
 
 def local(
@@ -73,15 +459,12 @@
     residual,
     unit_acts,
 ):
-    contract = (((0,), (0,)), ((), ()))
-    gradient_rows = lax.psum_scatter(
-        lax.dot_general(learn_hidden, out_cot, contract, preferred_element_type=jnp.float32).astype(
-            jnp.bfloat16
-        ),
-        "dp",
-        scatter_dimension=0,
-        tiled=True,
-    ).astype(jnp.float32)
+    attended = attend(queries, keys_cache, values_cache, keys_new, values_new, lengths)
+    stream = (residual.astype(jnp.float32) + attended.astype(jnp.float32)).astype(jnp.bfloat16)
+    mixed, gradient_rows = fused(
+        learn_hidden, out_cot, unit_acts.reshape(192, 1920), stream.reshape(192, 512), master, moment_one, moment_two
+    )
+    mixed = mixed.reshape(stream.shape)
     moment_one_next = beta_one * moment_one + (1.0 - beta_one) * gradient_rows
     moment_two_next = beta_two * moment_two + (1.0 - beta_two) * gradient_rows * gradient_rows
     first_hat = moment_one_next / (1.0 - beta_one**bias_steps)
@@ -89,23 +472,6 @@
     master_next = master - learn_rate * (
         first_hat / (jnp.sqrt(second_hat) + adam_eps) + decay_rate * master
     )
-    fresh_rows = master_next.astype(jnp.bfloat16)
-    attended = attend(queries, keys_cache, values_cache, keys_new, values_new, lengths)
-    stream = (residual.astype(jnp.float32) + attended.astype(jnp.float32)).astype(jnp.bfloat16)
-    step_count, row_count, share_width = stream.shape
-    unit_local = unit_acts.shape[3]
-    width = fresh_rows.shape[1]
-    mp_count = lax.axis_size("mp")
-    own_rows = fresh_rows.shape[0]
-    spread = fresh_rows.reshape(own_rows // mp_count, mp_count, width)
-    unit_pieces = lax.all_to_all(spread, "mp", split_axis=1, concat_axis=1, tiled=True)
-    acts_view = unit_acts.reshape(step_count * row_count, mp_count, unit_local // mp_count)
-    running = make_adder(acts_view, lax.all_gather(unit_pieces, "dp", axis=0, tiled=True))
-    partials = running.reshape(step_count, row_count, width)
-    summed = lax.psum_scatter(
-        partials.astype(jnp.bfloat16), "mp", scatter_dimension=2, tiled=True
-    ).astype(jnp.float32)
-    mixed = (stream.astype(jnp.float32) + summed).astype(jnp.bfloat16)
     return (mixed, master_next, moment_one_next, moment_two_next)
 
 

time: 405 us -> 156 us (0.39)
  waiting for transfers between devices: 323 us -> 0 us
  Pallas kernels: 0 us -> 134 us
  matrix products: 29.2 us -> 4.73 us
  blocking collectives: 21.2 us -> 0 us
  between operations: 13.9 us -> 0.75 us
    reduce_scatter x2 -> x0, waiting for transfers between devices: 242 us -> none  [the longest x1 175 us: local(): lax.psum_scatter(lax.dot_general(learn_hidden, out_cot, contract, preferr...]
    pallas_call x0 -> x1, Pallas kernels: none -> 134 us  [fused(): pl.pallas_call(fused_kernel, out_shape=(jax.ShapeDtypeStruct((192, 512),...]
    all_gather x1 -> x0, waiting for transfers between devices: 80.7 us -> none  [local(): lax.all_gather(unit_pieces, 'dp', axis=0, tiled=True)]
    dot_general x2 -> x0, matrix products: 23.7 us -> none  [the longest x1 13.4 us: local(): lax.dot_general(learn_hidden, out_cot, contract, preferred_element_type=j...]
    all_to_all x1 -> x0, blocking collectives: 21.2 us -> none  [local(): lax.all_to_all(spread, 'mp', split_axis=1, concat_axis=1, tiled=True)]
    reshape x1 -> x0, other arithmetic: 6.65 us -> none  [local(): spread = fresh_rows.reshape(own_rows // mp_count, mp_count, width)]
    sub x0 -> x1, other arithmetic: none -> 6.44 us  [local(): master - learn_rate * (first_hat / (jnp.sqrt(second_hat) + adam_eps) + de...]
  transfers between devices with their start and end apart: 3 -> 0, of which waited for: 3 -> 0; matrix products, arithmetic and copies ran while one was open for 3% -> 0% of each run, Pallas kernels for 0% -> 0%
where the time goes in v3:
time: 156 us
  Pallas kernels  134 us (86%)
  other arithmetic  10.1 us (6%)
  local copies, waits for them, and re-layouts  6.06 us (4%)
  matrix products  4.73 us (3%)
    pallas_call x1, Pallas kernels, fused(): pl.pallas_call(fused_kernel, out_shape=(jax.ShapeDtypeStruct((192, 512),...  134 us
    sub x1, other arithmetic, local(): master - learn_rate * (first_hat / (jnp.sqrt(second_hat) + adam_eps) + de...  6.44 us

profile of v3, /device:TPU:0, one launch (start us, length us, event | category | flops | bytes accessed | tf_op | source)
XLA Modules:
  0.0 155.5 jit_solution(3917346311953651341)
XLA Ops:
  0.6 0.0 copy-start
  0.6 0.0 copy-start.5
  0.7 0.8 iota_compare_fusion
  1.5 1.0 reshape.128
  2.5 0.0 copy-done
  2.5 1.0 fusion.34
  3.6 0.0 copy-start.4
  3.6 0.0 copy-done.5
  3.6 1.9 %fusion.35 = (f32[4,48,4]{2,0,1:T(4,128)S(1)}, f32[4,48,1,4,4]{3,4,0,1,2:T(4,128)S(1)}) fusion(bf16[4,48,4,128]{3,2,1,0:T(4,128)(2,1)S(1)} %reshape.128, bf16[4,48,128,1]{2,1,0,3:T(8,128)(2,1)S(1)} %bitcast.60, pred[4,4]{1,0:T(4,128)(4,1)S(1)} %iota_compare_fusion.1), kind=kOutput, calls=%fused_computation.38 | convolution fusion | flops 794880 | bytes 261136 | tf_op jit(solution)/shard_map/trkgd,srkd->trkgs/dot_general | solution.py:425
  5.5 0.4 fusion.24
  5.8 0.6 fusion.23
  6.4 0.0 copy-done.4
  6.5 0.0 copy-start.6
  6.5 0.7 fusion.1
  7.2 0.1 copy-done.6
  7.3 1.2 fusion.14
  8.4 2.0 %reshape.133 = f32[4,48,512]{2,0,1:T(4,128)} reshape(f32[4,48,1,4,128]{4,3,0,1,2:T(4,128)} %fusion.14) | data formatting | bytes 786432 | tf_op jit(solution)/shard_map/convert_element_type | solution.py:463
  10.4 1.8 %fusion.22 = bf16[4,48,512]{2,1,0:T(8,128)(2,1)} fusion(f32[4,48,512]{2,0,1:T(4,128)} %reshape.133, bf16[4,48,512]{2,1,0:T(8,128)(2,1)} %param.24), kind=kLoop, calls=%fused_computation.20 | loop fusion | flops 294912 | bytes 786432 | tf_op jit(solution)/shard_map/convert_element_type | solution.py:463
  12.2 0.0 copy-done.1
  12.2 2.3 %copy.17 = bf16[1920,512]{1,0:T(8,128)(2,1)} copy(bf16[1920,512]{0,1:T(8,128)(2,1)S(1)} %bitcast.55) | data formatting | bytes 3932160 | tf_op jit(solution)/shard_map/transpose | solution.py:364
  14.5 133.9 %fused.1 = (bf16[192,512]{1,0:T(8,128)(2,1)}, f32[120,4096]{1,0:T(8,128)}) custom-call(bf16[8,240,512]{2,1,0:T(8,128)(2,1)} %bitcast.56, bf16[512,4096]{1,0:T(8,128)(2,1)} %cot.1, bf16[192,1920]{1,0:T(8,128)(2,1)} %bitcast.59, bf16[192,512]{1,0:T(8,128)(2,1)} %bitcast.58, f32[120,4096]{1,0:T(8,128)} %master.1, f32[120,4096]{1,0:T(8,128)} %first.1, ...), custom_call_target="tpu_custom_call" | custom-call | flops 11274289152 | bytes 20971520 | tf_op jit(solution)/shard_map/fused/pallas_call | solution.py:373
  148.4 6.4 %multiply_subtract_fusion = (f32[120,4096]{1,0:T(8,128)}, f32[120,4096]{1,0:T(8,128)}, f32[120,4096]{1,0:T(8,128)}) fusion(f32[120,4096]{1,0:T(8,128)S(1)} %copy-done.2, f32[120,4096]{1,0:T(8,128)} %get-tuple-element.7, f32[120,4096]{1,0:T(8,128)} %first.1, f32[120,4096]{1,0:T(8,128)} %second.1), kind=kLoop, calls=%fused_computation.2 | loop fusion | flops 7372800 | bytes 13762560 | tf_op jit(solution)/shard_map/sub | solution.py:472
  154.9 0.0 copy-done.3
  154.9 0.7 copy.51
  (7 shorter events, 0.1 us)
Async XLA Ops:
  0.6 1.9 %copy-start = (bf16[48,128,128]{2,1,0:T(8,128)(2,1)S(1)}, bf16[48,128,128]{2,1,0:T(8,128)(2,1)}, u32[]{:S(2)}) copy-start(bf16[48,128,128]{2,1,0:T(8,128)(2,1)} %param.19) | copy-start | bytes 4718596
  0.6 2.9 %copy-start.5 = (bf16[4,48,128]{2,1,0:T(8,128)(2,1)S(1)}, bf16[4,48,128]{2,1,0:T(8,128)(2,1)}, u32[]{:S(2)}) copy-start(bf16[4,48,128]{2,1,0:T(8,128)(2,1)} %param.21) | copy-start | bytes 147460
  3.6 2.9 %copy-start.4 = (bf16[48,128,128]{2,1,0:T(8,128)(2,1)S(1)}, bf16[48,128,128]{2,1,0:T(8,128)(2,1)}, u32[]{:S(2)}) copy-start(bf16[48,128,128]{2,1,0:T(8,128)(2,1)} %param.20) | copy-start | bytes 4718596
  6.5 0.8 copy-start.6
  7.3 5.0 %copy-start.1 = (bf16[512,1920]{1,0:T(8,128)(2,1)S(1)}, bf16[512,1920]{1,0:T(8,128)(2,1)}, u32[]{:S(2)}) copy-start(bf16[512,1920]{1,0:T(8,128)(2,1)} %param.13) | copy-start | bytes 5898244
  14.5 133.9 %copy-start.2 = (f32[120,4096]{1,0:T(8,128)S(1)}, f32[120,4096]{1,0:T(8,128)}, u32[]{:S(2)}) copy-start(f32[120,4096]{1,0:T(8,128)} %master.1) | copy-start | bytes 5898244
  148.4 6.4 %copy-start.3 = (bf16[192,512]{1,0:T(8,128)(2,1)S(1)}, bf16[192,512]{1,0:T(8,128)(2,1)}, u32[]{:S(2)}) copy-start(bf16[192,512]{1,0:T(8,128)(2,1)} %get-tuple-element.6) | copy-start | bytes 589828

commit v4 on v3

--- a/solution.py
+++ b/solution.py
@@ -14,14 +14,14 @@
 CHUNKS = 4
 KIND = (("Z", "Y"), ("Z", "Y"), ("Z", "Y"), ("Z", "Y"))
 ORDER = [
-    ("yc", 1, 1), ("zc", 0, 0), ("zm", 0, 0), ("zc", 2, 0), ("yc", 0, 1), ("ze", 0, 0), ("zc", 1, 0), ("ys", 1, 1),
-    ("zm", 2, 0), ("zm", 1, 0), ("ym", 1, 1), ("yc", 2, 1), ("ys", 0, 1), ("zf", 0, 0), ("ym", 0, 1), ("ye", 1, 1),
-    ("zc", 3, 0), ("ye", 0, 1), ("ze", 1, 0), ("ad", 0), ("zm", 3, 0), ("ys", 2, 1), ("ze", 2, 0), ("zf", 1, 0),
-    ("ym", 2, 1), ("ad", 1), ("ga", 0), ("yc", 3, 1), ("ga", 1), ("ze", 3, 0), ("ye", 2, 1), ("zf", 2, 0), ("gb", 0),
-    ("ad", 2), ("gb", 1), ("gc", 0), ("ys", 3, 1), ("mm", 0), ("ym", 3, 1), ("zf", 3, 0), ("gc", 1), ("ga", 2),
-    ("ye", 3, 1), ("f2", 0), ("ad", 3), ("gb", 2), ("mm", 1), ("ga", 3), ("f3", 0), ("gc", 2), ("mm", 2), ("gb", 3),
-    ("f2", 2), ("gc", 3), ("f4", 0), ("f2", 1), ("mm", 3), ("f3", 1), ("f2", 3), ("f3", 2), ("f4", 1), ("f3", 3),
-    ("f4", 2), ("f5", 0), ("f4", 3), ("f5", 1), ("f5", 2), ("f5", 3),
+    ("zc", 1, 0), ("yc", 1, 1), ("zc", 3, 0), ("yc", 0, 1), ("zm", 1, 0), ("zc", 0, 0), ("zm", 0, 0), ("zc", 2, 0),
+    ("ap",), ("ze", 0, 0), ("zm", 2, 0), ("yc", 2, 1), ("ys", 0, 1), ("ym", 0, 1), ("ys", 1, 1), ("at", 0),
+    ("ze", 1, 0), ("ye", 0, 1), ("zf", 0, 0), ("ym", 1, 1), ("zm", 3, 0), ("ye", 1, 1), ("ad", 0), ("ys", 2, 1),
+    ("at", 1), ("zf", 1, 0), ("ze", 2, 0), ("ym", 2, 1), ("ad", 1), ("ga", 0), ("ye", 2, 1), ("yc", 3, 1), ("at", 2),
+    ("zf", 2, 0), ("ze", 3, 0), ("ga", 1), ("ad", 2), ("gb", 0), ("gb", 1), ("gc", 0), ("ys", 3, 1), ("mm", 0),
+    ("ym", 3, 1), ("gc", 1), ("zf", 3, 0), ("ga", 2), ("ye", 3, 1), ("ad", 3), ("mm", 1), ("gb", 2), ("ga", 3),
+    ("at", 3), ("gc", 2), ("f2", 0), ("mm", 2), ("gb", 3), ("at", 4), ("f3", 0), ("f2", 2), ("gc", 3), ("f2", 1),
+    ("at", 5), ("mm", 3), ("f2", 3), ("f3", 1), ("f3", 2), ("f3", 3), ("f5", 2), ("f5", 0), ("f5", 1), ("f5", 3),
 ]
 beta_one = 0.9
 beta_two = 0.999
@@ -40,10 +40,11 @@
     return ((z * 2 + y_lo) * 2 + core, x * 2 + y_hi)
 
 
-def fused_kernel(ht, cot, acts, stream, master, first, second, out, grad,
+def fused_kernel(ht, cot, acts, queries, keys, values, keys_new, values_new, lengths, residual,
+                 master, first, second, out, grad,
                  hs, cs, zs1, zsb, zs2, zr1, zrb, zr2, zhold, zown, zys, zyr,
                  yys, yyr, ys1, ysb, ys2, yr1, yrb, yr2, yhold, yown, gbuf, gall, adam,
-                 wsend, wbuf, asend, abuf, part, r1, rb, s2, r2, q, u1, ub, v2, u2,
+                 wsend, wbuf, asend, abuf, part, r1, rb, s2, r2, q, ug, kbuf, vbuf, qbuf, nbuf, att,
                  loc_sem, send_sem, recv_sem):
     z, y_lo, core, x, y_hi = coords()
     y, mp, slot = y_hi * 2 + y_lo, x * 2 + y_hi, z * 2 + core
@@ -54,13 +55,13 @@
     sib = place(z, y_lo, 1 - core, x, y_hi)
     z_up, z_down = place((z + 1) % 4, y_lo, core, x, y_hi), place((z + 3) % 4, y_lo, core, x, y_hi)
     x_up, x_down = place(z, y_lo, core, (x + 1) % 4, y_hi), place(z, y_lo, core, (x + 3) % 4, y_hi)
-    y_up, y_down = at_y((y + 1) % 4), at_y((y + 3) % 4)
+    y_place = [at_y((y + d) % 4) for d in range(1, 4)]
     across = place(z, 1 - y_lo, core, x, y_hi)
     peers = [((x + i // 2) % 4, (y_hi + i % 2) % 2) for i in range(1, 8)]
     peer_place = [place(z, y_lo, core, px, py) for px, py in peers]
 
     barrier = pltpu.get_barrier_semaphore()
-    everyone = peer_place + [sib, z_up, z_down, y_up, y_down]
+    everyone = peer_place + [sib, z_up, z_down, y_place[0], y_place[2]]
     for other in everyone:
         pl.semaphore_signal(barrier, inc=1, device_id=other, device_id_type=MESHID)
     pl.semaphore_wait(barrier, len(everyone))
@@ -86,17 +87,37 @@
         copy.start()
         return copy
 
-    h_own = local(ht, hs.at[:, :, pl.ds(0, 512)])
-    h_sib = send(ht, hs.at[:, :, pl.ds(512, 512)], sib)
-    for k in range(4):
-        for h in range(2):
-            st["c", k, h] = []
-            for i in range(2):
-                mine = pl.ds(pl.multiple_of((4 * core + 2 * h + i) * 512 + k * 128, 128), 128)
-                theirs = pl.ds(pl.multiple_of((4 - 4 * core + 2 * h + i) * 512 + k * 128, 128), 128)
-                lanes = pl.ds(i * 128, 128)
-                st["c", k, h].append(send(cot.at[:, theirs], cs.at[k, h, pl.ds(512, 512), lanes], sib))
-                st["c", k, h].append(local(cot.at[:, mine], cs.at[k, h, pl.ds(0, 512), lanes]))
+    zp, zm, zf = (z + 1) % 4, (z + 3) % 4, (z + 2) % 4
+    offset = [2, 1, 3, 0]
+
+    def share_hidden(i):
+        blocks = pl.ds(((z + offset[i]) % 4) * 2, 2)
+        st["h", i] = [send(ht.at[blocks], hs.at[blocks, :, pl.ds(512, 512)], sib),
+                      local(ht.at[blocks], hs.at[blocks, :, pl.ds(0, 512)])]
+
+    def share_cotangent(k, h):
+        st["c", k, h] = []
+        for i in range(2):
+            mine = pl.ds(pl.multiple_of((4 * core + 2 * h + i) * 512 + k * 128, 128), 128)
+            theirs = pl.ds(pl.multiple_of((4 - 4 * core + 2 * h + i) * 512 + k * 128, 128), 128)
+            lanes = pl.ds(i * 128, 128)
+            st["c", k, h].append(send(cot.at[:, theirs], cs.at[k, h, pl.ds(512, 512), lanes], sib))
+            st["c", k, h].append(local(cot.at[:, mine], cs.at[k, h, pl.ds(0, 512), lanes]))
+
+    first_use = [where for name, *where in ORDER if name in ("yc", "zc")]
+    share_hidden(0)
+    share_cotangent(*first_use[0])
+    for i in range(1, 4):
+        share_hidden(i)
+    for where in first_use[1:]:
+        share_cotangent(*where)
+    st["kv"] = [local(keys, kbuf), local(values, vbuf)]
+
+    def hidden(i):
+        if ("got", i) not in st:
+            st["got", i] = True
+            st["h", i][0].wait_recv()
+            st["h", i][1].wait()
 
     def adam_fetch(k):
         for b in range(8):
@@ -120,30 +141,29 @@
     swap = send(asend.at[1 - y_lo], abuf.at[y_lo], across)
     abuf[y_lo] = asend[y_lo]
 
-    h_own.wait()
-    h_sib.wait_recv()
-
     def ready(k, h):
         for i in range(2):
             st["c", k, h][2 * i].wait_recv()
             st["c", k, h][2 * i + 1].wait()
 
-    zp, zm, zf = (z + 1) % 4, (z + 3) % 4, (z + 2) % 4
-
     def ring_start(key, term, s1, sb, r1, rb, hold, own):
+        hidden(0)
         p = term(zf)
         s1[0] = p[:, :128].astype(bf16)
         s1[1] = p[:, 128:].astype(bf16)
         st["r1", key] = [send(s1.at[0], r1.at[0], z_up), send(s1.at[1], r1.at[1], z_down)]
+        hidden(1)
         p = term(zp)
         sb[0] = p[:, 128:].astype(bf16)
         b0 = send(sb.at[0], rb.at[0], z_up)
         hold[0] = p[:, :128].astype(hold.dtype)
+        hidden(2)
         p = term(zm)
         sb[1] = p[:, :128].astype(bf16)
         b1 = send(sb.at[1], rb.at[1], z_down)
         hold[1] = p[:, 128:].astype(hold.dtype)
         st["rb", key] = [b0, b1]
+        hidden(3)
         own[...] = term(z)
 
     def ring_mid(key, s2, r1, r2, hold):
@@ -207,6 +227,8 @@
     def yc(k, h):
         n = index[k, h]
         ready(k, h)
+        for i in range(4):
+            hidden(i)
 
         def body(zb, carry):
             yys[n, zb] = jnp.dot(hs[2 * zb + 1 - y_lo], cs[k, h], preferred_element_type=f32).astype(bf16)
@@ -245,8 +267,7 @@
             for i in range(3):
                 st["m", k, b, i].wait()
             g = gall[k, b // 4, (b // 2) % 2, :, (b % 2) * 128:(b % 2 + 1) * 128]
-            st["o", k, b] = local(gall.at[k, b // 4, (b // 2) % 2, :, pl.ds((b % 2) * 128, 128)],
-                                  grad.at[:, pl.ds(b * 512 + k * 128, 128)])
+            grad[:, b * 512 + k * 128:b * 512 + (k + 1) * 128] = g
             m = adam[k % 2, 0, b]
             one = beta_one * adam[k % 2, 1, b] + (1.0 - beta_one) * g
             two = beta_two * adam[k % 2, 2, b] + (1.0 - beta_two) * g * g
@@ -324,43 +345,69 @@
         st["fb", k][0].wait_recv()
         st["f2", k][1].wait_recv()
         q[k, pl.ds(2, 2)] = (part[k, x, pl.ds(2, 2)].astype(f32) + rb[k, 0].astype(f32) + r2[k, 1].astype(f32)).astype(bf16)
-        far, above, below = (y + 2) % 4, (y + 1) % 4, (y + 3) % 4
-        lo, hi = pl.ds(0, 96), pl.ds(96, 96)
-        st["g1", k] = [send(q.at[k, far, lo], u1.at[k, 0], y_up), send(q.at[k, far, hi], u1.at[k, 1], y_down)]
-        st["gb", k] = [send(q.at[k, above, hi], ub.at[k, 0], y_up), send(q.at[k, below, lo], ub.at[k, 1], y_down)]
-
-    def f4(k):
-        above, below = (y + 1) % 4, (y + 3) % 4
-        st["g1", k][0].wait_recv()
-        v2[k, 0] = (q[k, above, pl.ds(0, 96)].astype(f32) + u1[k, 0].astype(f32)).astype(bf16)
-        a = send(v2.at[k, 0], u2.at[k, 0], y_up)
-        st["g1", k][1].wait_recv()
-        v2[k, 1] = (q[k, below, pl.ds(96, 96)].astype(f32) + u1[k, 1].astype(f32)).astype(bf16)
-        st["g2", k] = [a, send(v2.at[k, 1], u2.at[k, 1], y_down)]
+        st["g", k] = [send(q.at[k, (y + d) % 4], ug.at[k, d - 1], y_place[d - 1]) for d in range(1, 4)]
 
     def f5(k):
         cols = pl.ds(k * 128, 128)
-        st["gb", k][1].wait_recv()
-        st["g2", k][0].wait_recv()
-        lo = q[k, y, pl.ds(0, 96)].astype(f32) + ub[k, 1].astype(f32) + u2[k, 0].astype(f32)
-        out[pl.ds(0, 96), cols] = (stream[pl.ds(0, 96), cols].astype(f32) + lo).astype(bf16)
-        st["gb", k][0].wait_recv()
-        st["g2", k][1].wait_recv()
-        hi = q[k, y, pl.ds(96, 96)].astype(f32) + ub[k, 0].astype(f32) + u2[k, 1].astype(f32)
-        out[pl.ds(96, 96), cols] = (stream[pl.ds(96, 96), cols].astype(f32) + hi).astype(bf16)
+        total = q[k, y].astype(f32)
+        for i in range(3):
+            st["g", k][i].wait_recv()
+            total = total + ug[k, i].astype(f32)
+        attended = att[:, k].reshape(192, 128).astype(bf16).astype(f32)
+        stream = (residual[:, cols].astype(f32) + attended).astype(bf16)
+        out[:, cols] = (stream.astype(f32) + total).astype(bf16)
+
+    def ap():
+        for g in range(HEADS // KV_HEADS):
+            qbuf[:, g] = queries[:, :, g * 128:(g + 1) * 128].astype(f32)
+        nbuf[0] = keys_new[...].astype(f32)
+        nbuf[1] = values_new[...].astype(f32)
+        for copy in st["kv"]:
+            copy.wait()
+
+    def at(i):
+        position = lax.broadcasted_iota(jnp.int32, (16, 128), 1)
+        when = lax.broadcasted_iota(jnp.int32, (16, 1), 0) // 4
+        heads = HEADS // KV_HEADS
+
+        def rows(n, carry):
+            for j in range(4):
+                r = i * 8 + n * 4 + j
+                qr = jnp.concatenate(
+                    [qbuf[t, g, pl.ds(r, 1), :] for t in range(4) for g in range(heads)], axis=0)
+                cached = lax.dot_general(qr.astype(bf16), kbuf[r], (((1,), (1,)), ((), ())),
+                                         preferred_element_type=f32) * HEAD_DIM ** (-0.5)
+                cached = jnp.where(position < lengths[r], cached, -jnp.inf)
+                fresh = []
+                for s in range(4):
+                    score = jnp.sum(qr * nbuf[0, s, pl.ds(r, 1), :], axis=1, keepdims=True) * HEAD_DIM ** (-0.5)
+                    fresh.append(jnp.where(when >= s, score, -jnp.inf))
+                highest = jnp.max(cached, axis=1, keepdims=True)
+                for score in fresh:
+                    highest = jnp.maximum(highest, score)
+                cached = jnp.exp(cached - highest)
+                fresh = [jnp.exp(score - highest) for score in fresh]
+                total = jnp.sum(cached, axis=1, keepdims=True) + (fresh[0] + fresh[1]) + (fresh[2] + fresh[3])
+                result = jnp.dot((cached / total).astype(bf16), vbuf[r], preferred_element_type=f32)
+                for s in range(4):
+                    weight = (fresh[s] / total).astype(bf16).astype(f32)
+                    result = result + weight * nbuf[1, s, pl.ds(r, 1), :]
+                for t in range(4):
+                    for g in range(heads):
+                        att[t, g, pl.ds(r, 1), :] = result[t * heads + g:t * heads + g + 1]
+            return carry
+
+        lax.fori_loop(0, 2, rows, 0)
 
     steps = {"zc": zc, "zm": zm_, "ze": ze, "zf": zf_, "yc": yc, "ys": ys, "ym": ym, "ye": ye, "ad": ad,
-             "ga": ga, "gb": gb, "gc": gc, "mm": mm, "f2": f2, "f3": f3, "f4": f4, "f5": f5}
+             "ga": ga, "gb": gb, "gc": gc, "mm": mm, "f2": f2, "f3": f3, "f5": f5, "ap": ap, "at": at}
     for name, *where in ORDER:
         steps[name](*where)
-    for k in range(4):
-        for b in range(8):
-            st["o", k, b].wait()
     for copy in sends:
         copy.wait_send()
 
 
-def fused(learn_hidden, out_cot, acts, stream, master, first, second):
+def fused(learn_hidden, out_cot, acts, queries, keys, values, keys_new, values_new, lengths, residual, master, first, second):
     ht = learn_hidden.T.reshape(8, 240, 512)
     kinds = [a for pair in KIND for a in pair]
     nz, ny = max(kinds.count("Z"), 1), max(kinds.count("Y"), 1)
@@ -368,14 +415,16 @@
     def ring(n, r):
         return [pltpu.VMEM((n, 2, r, 128), bf16)] * 7 + [pltpu.VMEM((n, r, 256), f32)]
 
-    copies = 1 + 16 + 1 + 8 * 8 + 4 * 27
-    locals_ = 1 + 16 + 4 * (24 + 8 + 1)
+    copies = 4 + 16 + 1 + 8 * 8 + 4 * 24
+    locals_ = 4 + 16 + 2 + 4 * (24 + 1)
     return pl.pallas_call(
         fused_kernel,
         out_shape=(jax.ShapeDtypeStruct((192, 512), bf16), jax.ShapeDtypeStruct((120, 4096), f32)),
         in_specs=[pl.BlockSpec(memory_space=pl.ANY)] * 2 + [pl.BlockSpec(memory_space=pltpu.VMEM)] * 2
+        + [pl.BlockSpec(memory_space=pl.ANY)] * 2 + [pl.BlockSpec(memory_space=pltpu.VMEM)] * 2
+        + [pl.BlockSpec(memory_space=pltpu.SMEM), pl.BlockSpec(memory_space=pltpu.VMEM)]
         + [pl.BlockSpec(memory_space=pl.ANY)] * 3,
-        out_specs=(pl.BlockSpec(memory_space=pltpu.VMEM), pl.BlockSpec(memory_space=pl.ANY)),
+        out_specs=(pl.BlockSpec(memory_space=pltpu.VMEM),) * 2,
         scratch_shapes=[
             pltpu.VMEM((8, 240, 1024), bf16),
             pltpu.VMEM((4, 2, 1024, 256), bf16),
@@ -395,7 +444,12 @@
             pltpu.VMEM((4, 4, 4, 192, 128), bf16),
             *[pltpu.VMEM((4, 2, 2, 192, 128), bf16)] * 4,
             pltpu.VMEM((4, 4, 192, 128), bf16),
-            *[pltpu.VMEM((4, 2, 96, 128), bf16)] * 4,
+            pltpu.VMEM((4, 3, 192, 128), bf16),
+            pltpu.VMEM((48, 128, 128), bf16),
+            pltpu.VMEM((48, 128, 128), bf16),
+            pltpu.VMEM((4, 4, 48, 128), f32),
+            pltpu.VMEM((2, 4, 48, 128), f32),
+            pltpu.VMEM((4, 4, 48, 128), f32),
             pltpu.SemaphoreType.DMA((locals_,)),
             pltpu.SemaphoreType.DMA((copies,)),
             pltpu.SemaphoreType.DMA((copies,)),
@@ -403,45 +457,7 @@
         compiler_params=pltpu.CompilerParams(collective_id=0, has_side_effects=True, vmem_limit_bytes=60 * 2**20),
         cost_estimate=pl.CostEstimate(flops=11274289152, bytes_accessed=20 * 2**20, transcendentals=0),
         name="fused",
-    )(ht, out_cot, acts, stream, master, first, second)
-
-
-def attend(queries, keys_cache, values_cache, keys_new, values_new, lengths):
-    step_count, row_count, row_width = queries.shape
-    cache_len = keys_cache.shape[1]
-    kv_local = keys_cache.shape[2] // HEAD_DIM
-    per_group = HEADS // KV_HEADS
-    query_heads = queries.reshape(step_count, row_count, kv_local, per_group, HEAD_DIM)
-    cache_keys = keys_cache.reshape(row_count, cache_len, kv_local, HEAD_DIM)
-    cache_values = values_cache.reshape(row_count, cache_len, kv_local, HEAD_DIM)
-    new_keys = keys_new.reshape(step_count, row_count, kv_local, HEAD_DIM)
-    new_values = values_new.reshape(step_count, row_count, kv_local, HEAD_DIM)
-    score_scale = HEAD_DIM ** (-0.5)
-    cache_scores = (
-        jnp.einsum("trkgd,rlkd->trkgl", query_heads, cache_keys, preferred_element_type=jnp.float32)
-        * score_scale
-    )
-    new_scores = (
-        jnp.einsum("trkgd,srkd->trkgs", query_heads, new_keys, preferred_element_type=jnp.float32)
-        * score_scale
-    )
-    visible = jnp.arange(cache_len)[None, :] < lengths[:, None]
-    causal = jnp.arange(step_count)[:, None] >= jnp.arange(step_count)[None, :]
-    cache_scores = jnp.where(visible[None, :, None, None, :], cache_scores, -jnp.inf)
-    new_scores = jnp.where(causal[:, None, None, None, :], new_scores, -jnp.inf)
-    highest = jnp.maximum(jnp.max(cache_scores, axis=-1), jnp.max(new_scores, axis=-1))
-    cache_exp = jnp.exp(cache_scores - highest[..., None])
-    new_exp = jnp.exp(new_scores - highest[..., None])
-    exp_total = jnp.sum(cache_exp, axis=-1) + jnp.sum(new_exp, axis=-1)
-    cache_probs = (cache_exp / exp_total[..., None]).astype(jnp.bfloat16)
-    new_probs = (new_exp / exp_total[..., None]).astype(jnp.bfloat16)
-    mixed_heads = jnp.einsum(
-        "trkgl,rlkd->trkgd", cache_probs, cache_values, preferred_element_type=jnp.float32
-    )
-    mixed_heads = mixed_heads + jnp.einsum(
-        "trkgs,srkd->trkgd", new_probs, new_values, preferred_element_type=jnp.float32
-    )
-    return mixed_heads.reshape(step_count, row_count, row_width).astype(jnp.bfloat16)
+    )(ht, out_cot, acts, queries, keys, values, keys_new, values_new, lengths, residual, master, first, second)
 
 
 def local(
@@ -459,12 +475,11 @@
     residual,
     unit_acts,
 ):
-    attended = attend(queries, keys_cache, values_cache, keys_new, values_new, lengths)
-    stream = (residual.astype(jnp.float32) + attended.astype(jnp.float32)).astype(jnp.bfloat16)
     mixed, gradient_rows = fused(
-        learn_hidden, out_cot, unit_acts.reshape(192, 1920), stream.reshape(192, 512), master, moment_one, moment_two
+        learn_hidden, out_cot, unit_acts.reshape(192, 1920), queries, keys_cache, values_cache, keys_new, values_new,
+        lengths, residual.reshape(192, 512), master, moment_one, moment_two
     )
-    mixed = mixed.reshape(stream.shape)
+    mixed = mixed.reshape(residual.shape)
     moment_one_next = beta_one * moment_one + (1.0 - beta_one) * gradient_rows
     moment_two_next = beta_two * moment_two + (1.0 - beta_two) * gradient_rows * gradient_rows
     first_hat = moment_one_next / (1.0 - beta_one**bias_steps)

time: 156 us -> 148 us (0.949)
  matrix products: 4.73 us -> 0 us
  other arithmetic: 10.1 us -> 5.84 us
  Pallas kernels: 134 us -> 136 us
    dot_general x4 -> x0, matrix products: 4.73 us -> none  [the longest x1 1.85 us: attend(): jnp.einsum('trkgd,srkd->trkgs', query_heads, new_keys, preferred_element_...]
    pallas_call x1, Pallas kernels: 134 us -> 136 us  [fused(): pl.pallas_call(fused_kernel, out_shape=(jax.ShapeDtypeStruct((192, 512),...]
    convert_element_type x1 -> x0, local copies, waits for them, and re-layouts: 1.97 us -> none  [local(): attended.astype(jnp.float32)]
    convert_element_type x1 -> x0, other arithmetic: 1.85 us -> none  [local(): (residual.astype(jnp.float32) + attended.astype(jnp.float32)).astype(jnp....]
    transpose x1, local copies, waits for them, and re-layouts: 2.29 us -> 3.98 us  [fused(): ht = learn_hidden.T.reshape(8, 240, 512)]
where the time goes in v4:
time: 148 us
  Pallas kernels  136 us (92%)
  other arithmetic  5.84 us (4%)
  local copies, waits for them, and re-layouts  4.67 us (3%)
    pallas_call x1, Pallas kernels, fused(): pl.pallas_call(fused_kernel, out_shape=(jax.ShapeDtypeStruct((192, 512),...  136 us
    sub x1, other arithmetic, local(): master - learn_rate * (first_hat / (jnp.sqrt(second_hat) + adam_eps) + de...  5.84 us
    transpose x1, local copies, waits for them, and re-layouts, fused(): ht = learn_hidden.T.reshape(8, 240, 512)  3.98 us

profile of v4, /device:TPU:0, one launch (start us, length us, event | category | flops | bytes accessed | tf_op | source)
XLA Modules:
  0.0 147.6 jit_solution(7484075595147752907)
XLA Ops:
  0.6 4.0 %copy.17 = bf16[1920,512]{1,0:T(8,128)(2,1)} copy(bf16[1920,512]{0,1:T(8,128)(2,1)} %bitcast.5) | data formatting | bytes 3932160 | tf_op jit(solution)/shard_map/transpose | solution.py:411
  4.6 0.0 copy-start
  4.6 0.0 copy-start.1
  4.6 136.4 %fused.1 = (bf16[192,512]{1,0:T(8,128)(2,1)}, f32[120,4096]{1,0:T(8,128)}) custom-call(bf16[8,240,512]{2,1,0:T(8,128)(2,1)} %bitcast.6, bf16[512,4096]{1,0:T(8,128)(2,1)} %cot.1, bf16[192,1920]{1,0:T(8,128)(2,1)} %bitcast.8, bf16[4,48,512]{2,1,0:T(8,128)(2,1)} %queries.1, bf16[48,128,128]{2,1,0:T(8,128)(2,1)} %keys.1, bf16[48,128,128]{2,1,0:T(8,128)(2,1)} %values.1, ...), custom_call_target="tpu_custom_call" | custom-call | flops 11274289152 | bytes 20971520 | tf_op jit(solution)/shard_map/fused/pallas_call | solution.py:420
  141.0 0.0 copy-done
  141.0 0.0 copy-done.1
  141.0 0.0 copy-start.2
  141.0 5.8 %multiply_subtract_fusion = (f32[120,4096]{1,0:T(8,128)}, f32[120,4096]{1,0:T(8,128)}, f32[120,4096]{1,0:T(8,128)}) fusion(f32[120,4096]{1,0:T(8,128)S(1)} %copy-done, f32[120,4096]{1,0:T(8,128)} %get-tuple-element.7, f32[120,4096]{1,0:T(8,128)S(1)} %copy-done.1, f32[120,4096]{1,0:T(8,128)} %second.1), kind=kLoop, calls=%fused_computation.2 | loop fusion | flops 7372800 | bytes 13762560 | tf_op jit(solution)/shard_map/sub | solution.py:487
  146.9 0.0 copy-done.2
  146.9 0.7 copy.19
Async XLA Ops:
  4.6 136.4 %copy-start = (f32[120,4096]{1,0:T(8,128)S(1)}, f32[120,4096]{1,0:T(8,128)}, u32[]{:S(2)}) copy-start(f32[120,4096]{1,0:T(8,128)} %master.1) | copy-start | bytes 5898244
  4.6 136.4 %copy-start.1 = (f32[120,4096]{1,0:T(8,128)S(1)}, f32[120,4096]{1,0:T(8,128)}, u32[]{:S(2)}) copy-start(f32[120,4096]{1,0:T(8,128)} %first.1) | copy-start | bytes 5898244
  141.0 5.9 %copy-start.2 = (bf16[192,512]{1,0:T(8,128)(2,1)S(1)}, bf16[192,512]{1,0:T(8,128)(2,1)}, u32[]{:S(2)}) copy-start(bf16[192,512]{1,0:T(8,128)(2,1)} %get-tuple-element.6) | copy-start | bytes 589828

commit v5 on v4

--- a/solution.py
+++ b/solution.py
@@ -12,16 +12,19 @@
 KV_HEADS = 8
 HEAD_DIM = 128
 CHUNKS = 4
-KIND = (("Z", "Y"), ("Z", "Y"), ("Z", "Y"), ("Z", "Y"))
+KIND = (("Z", "Z"), ("Z", "B"), ("B", "B"), ("B", "B"))
+NEAR = 192
 ORDER = [
-    ("zc", 1, 0), ("yc", 1, 1), ("zc", 3, 0), ("yc", 0, 1), ("zm", 1, 0), ("zc", 0, 0), ("zm", 0, 0), ("zc", 2, 0),
-    ("ap",), ("ze", 0, 0), ("zm", 2, 0), ("yc", 2, 1), ("ys", 0, 1), ("ym", 0, 1), ("ys", 1, 1), ("at", 0),
-    ("ze", 1, 0), ("ye", 0, 1), ("zf", 0, 0), ("ym", 1, 1), ("zm", 3, 0), ("ye", 1, 1), ("ad", 0), ("ys", 2, 1),
-    ("at", 1), ("zf", 1, 0), ("ze", 2, 0), ("ym", 2, 1), ("ad", 1), ("ga", 0), ("ye", 2, 1), ("yc", 3, 1), ("at", 2),
-    ("zf", 2, 0), ("ze", 3, 0), ("ga", 1), ("ad", 2), ("gb", 0), ("gb", 1), ("gc", 0), ("ys", 3, 1), ("mm", 0),
-    ("ym", 3, 1), ("gc", 1), ("zf", 3, 0), ("ga", 2), ("ye", 3, 1), ("ad", 3), ("mm", 1), ("gb", 2), ("ga", 3),
-    ("at", 3), ("gc", 2), ("f2", 0), ("mm", 2), ("gb", 3), ("at", 4), ("f3", 0), ("f2", 2), ("gc", 3), ("f2", 1),
-    ("at", 5), ("mm", 3), ("f2", 3), ("f3", 1), ("f3", 2), ("f3", 3), ("f5", 2), ("f5", 0), ("f5", 1), ("f5", 3),
+    ("zc", 0, 1), ("bs", 1, 1), ("bs", 2, 0), ("zc", 1, 0), ("bs", 2, 1), ("hf", 0), ("bs", 3, 1), ("zm", 0, 1),
+    ("ac",), ("ap",), ("zm", 1, 0), ("zc", 0, 0), ("ze", 0, 1), ("bf", 1, 1), ("hf", 1), ("hf", 2), ("hf", 3),
+    ("zm", 0, 0), ("bf", 2, 0), ("at", 0), ("bz", 1, 1), ("bf", 2, 1), ("bf", 3, 1), ("bs", 3, 0), ("bz", 2, 0),
+    ("ze", 0, 0), ("zf", 0, 1), ("ym", 1, 1), ("bz", 2, 1), ("ym", 2, 0), ("bf", 3, 0), ("ze", 1, 0), ("zf", 0, 0),
+    ("bz", 3, 1), ("ad", 0), ("ym", 2, 1), ("bz", 3, 0), ("ye", 2, 0), ("ye", 1, 1), ("zf", 1, 0), ("ga", 0),
+    ("at", 1), ("ym", 3, 1), ("ye", 2, 1), ("ad", 1), ("ad", 2), ("ym", 3, 0), ("sw",), ("gb", 0), ("ga", 1),
+    ("ye", 3, 0), ("gc", 0), ("at", 2), ("ye", 3, 1), ("ga", 2), ("ad", 3), ("gb", 1), ("at", 3), ("mm", 0),
+    ("gb", 2), ("f2", 0), ("ga", 3), ("gc", 1), ("mm", 1), ("gc", 2), ("mm", 2), ("f2", 1), ("gb", 3), ("f2", 2),
+    ("gc", 3), ("at", 4), ("mm", 3), ("f3", 0), ("at", 5), ("f3", 1), ("f3", 2), ("f5", 0), ("f2", 3), ("f5", 1),
+    ("f3", 3), ("f5", 2), ("f5", 3),
 ]
 beta_one = 0.9
 beta_two = 0.999
@@ -40,10 +43,10 @@
     return ((z * 2 + y_lo) * 2 + core, x * 2 + y_hi)
 
 
-def fused_kernel(ht, cot, acts, queries, keys, values, keys_new, values_new, lengths, residual,
+def fused_kernel(hidden_in, cot, acts, queries, keys, values, keys_new, values_new, lengths, residual,
                  master, first, second, out, grad,
                  hs, cs, zs1, zsb, zs2, zr1, zrb, zr2, zhold, zown, zys, zyr,
-                 yys, yyr, ys1, ysb, ys2, yr1, yrb, yr2, yhold, yown, gbuf, gall, adam,
+                 hraw, ho, co, ys1, ysb, ys2, yr1, yrb, yr2, yhold, yown, gbuf, gall, adam,
                  wsend, wbuf, asend, abuf, part, r1, rb, s2, r2, q, ug, kbuf, vbuf, qbuf, nbuf, att,
                  loc_sem, send_sem, recv_sem):
     z, y_lo, core, x, y_hi = coords()
@@ -59,12 +62,6 @@
     across = place(z, 1 - y_lo, core, x, y_hi)
     peers = [((x + i // 2) % 4, (y_hi + i % 2) % 2) for i in range(1, 8)]
     peer_place = [place(z, y_lo, core, px, py) for px, py in peers]
-
-    barrier = pltpu.get_barrier_semaphore()
-    everyone = peer_place + [sib, z_up, z_down, y_place[0], y_place[2]]
-    for other in everyone:
-        pl.semaphore_signal(barrier, inc=1, device_id=other, device_id_type=MESHID)
-    pl.semaphore_wait(barrier, len(everyone))
 
     count = [0, 0]
     sends = []
@@ -87,13 +84,35 @@
         copy.start()
         return copy
 
+    other = at_y((y + 3 + 2 * y_lo) % 4)
+    raw = local(hidden_in, hraw)
+    barrier = pltpu.get_barrier_semaphore()
+    everyone = peer_place + [sib, z_up, z_down, y_place[0], y_place[2]]
+    for device in everyone:
+        pl.semaphore_signal(barrier, inc=1, device_id=device, device_id_type=MESHID)
     zp, zm, zf = (z + 1) % 4, (z + 3) % 4, (z + 2) % 4
     offset = [2, 1, 3, 0]
 
+    def turn_hidden(i):
+        row = lax.broadcasted_iota(jnp.int32, (240, 384), 0)
+        lane = lax.broadcasted_iota(jnp.int32, (240, 384), 1)
+        for yl in range(2):
+            b = ((z + offset[i]) % 4) * 2 + yl
+            start = jnp.minimum(b * 240 // 128 * 128, 1536)
+            e = jnp.where(lane - (b * 240 - start) == row, 1.0, 0.0).astype(bf16)
+            window = hraw[:, pl.ds(pl.multiple_of(start, 128), 384)]
+            turned = lax.dot_general(e, window, (((1,), (1,)), ((), ())), preferred_element_type=f32)
+            hs[b, :, pl.ds(0, 512)] = turned.astype(bf16)
+
     def share_hidden(i):
-        blocks = pl.ds(((z + offset[i]) % 4) * 2, 2)
-        st["h", i] = [send(ht.at[blocks], hs.at[blocks, :, pl.ds(512, 512)], sib),
-                      local(ht.at[blocks], hs.at[blocks, :, pl.ds(0, 512)])]
+        zb = (z + offset[i]) % 4
+        blocks = pl.ds(zb * 2, 2)
+        st["h", i] = send(hs.at[blocks, :, pl.ds(0, 512)], hs.at[blocks, :, pl.ds(512, 512)], sib)
+        st["hy", i] = send(hs.at[zb * 2 + 1 - y_lo, :, pl.ds(0, 512)], ho.at[i, :, pl.ds(0, 512)], across)
+
+    def hf(i):
+        st["hy", i].wait_recv()
+        st["hs", i] = send(ho.at[i, :, pl.ds(0, 512)], ho.at[i, :, pl.ds(512, 512)], sib)
 
     def share_cotangent(k, h):
         st["c", k, h] = []
@@ -104,10 +123,14 @@
             st["c", k, h].append(send(cot.at[:, theirs], cs.at[k, h, pl.ds(512, 512), lanes], sib))
             st["c", k, h].append(local(cot.at[:, mine], cs.at[k, h, pl.ds(0, 512), lanes]))
 
-    first_use = [where for name, *where in ORDER if name in ("yc", "zc")]
+    first_use = [where for name, *where in ORDER if name in ("bs", "zc")]
+    raw.wait()
+    turn_hidden(0)
+    pl.semaphore_wait(barrier, len(everyone))
     share_hidden(0)
     share_cotangent(*first_use[0])
     for i in range(1, 4):
+        turn_hidden(i)
         share_hidden(i)
     for where in first_use[1:]:
         share_cotangent(*where)
@@ -116,8 +139,7 @@
     def hidden(i):
         if ("got", i) not in st:
             st["got", i] = True
-            st["h", i][0].wait_recv()
-            st["h", i][1].wait()
+            st["h", i].wait_recv()
 
     def adam_fetch(k):
         for b in range(8):
@@ -126,20 +148,23 @@
 
     adam_fetch(0)
 
-    unit = lax.broadcasted_iota(jnp.int32, (384, 256), 0)
-    lane = lax.broadcasted_iota(jnp.int32, (384, 256), 1)
-    owner = (lane % 128) // 16
-    target = ((owner // 2) * 4 + (lane // 128) * 2 + owner % 2) * 15 + lane % 16
-    target = jnp.where(lane % 16 < 15, target, -1000)
-    for b in range(8):
-        start, shift = (b * 240) // 128 * 128, (b * 240) % 128
-        depth = 256 if shift + 240 <= 256 else 384
-        e = jnp.where(unit[:depth] - shift == target[:depth], 1.0, 0.0).astype(bf16)
-        a = jnp.dot(acts[:, start:start + depth], e, preferred_element_type=f32).astype(bf16)
-        asend[0, :, b * 128:(b + 1) * 128] = a[:, :128]
-        asend[1, :, b * 128:(b + 1) * 128] = a[:, 128:]
-    swap = send(asend.at[1 - y_lo], abuf.at[y_lo], across)
-    abuf[y_lo] = asend[y_lo]
+    def ac():
+        unit = lax.broadcasted_iota(jnp.int32, (384, 256), 0)
+        lane = lax.broadcasted_iota(jnp.int32, (384, 256), 1)
+        owner = (lane % 128) // 16
+        target = ((owner // 2) * 4 + (lane // 128) * 2 + owner % 2) * 15 + lane % 16
+        target = jnp.where(lane % 16 < 15, target, -1000)
+        for b in range(8):
+            start, shift = (b * 240) // 128 * 128, (b * 240) % 128
+            depth = 256 if shift + 240 <= 256 else 384
+            e = jnp.where(unit[:depth] - shift == target[:depth], 1.0, 0.0).astype(bf16)
+            a = jnp.dot(acts[:, start:start + depth], e, preferred_element_type=f32).astype(bf16)
+            asend[0, :, b * 128:(b + 1) * 128] = a[:, :128]
+            asend[1, :, b * 128:(b + 1) * 128] = a[:, 128:]
+        abuf[y_lo] = asend[y_lo]
+
+    def sw():
+        st["sw"] = send(asend.at[1 - y_lo], abuf.at[y_lo], across)
 
     def ready(k, h):
         for i in range(2):
@@ -148,23 +173,23 @@
 
     def ring_start(key, term, s1, sb, r1, rb, hold, own):
         hidden(0)
-        p = term(zf)
+        p = term(0, zf)
         s1[0] = p[:, :128].astype(bf16)
         s1[1] = p[:, 128:].astype(bf16)
         st["r1", key] = [send(s1.at[0], r1.at[0], z_up), send(s1.at[1], r1.at[1], z_down)]
         hidden(1)
-        p = term(zp)
+        p = term(1, zp)
         sb[0] = p[:, 128:].astype(bf16)
         b0 = send(sb.at[0], rb.at[0], z_up)
         hold[0] = p[:, :128].astype(hold.dtype)
         hidden(2)
-        p = term(zm)
+        p = term(2, zm)
         sb[1] = p[:, :128].astype(bf16)
         b1 = send(sb.at[1], rb.at[1], z_down)
         hold[1] = p[:, 128:].astype(hold.dtype)
         st["rb", key] = [b0, b1]
         hidden(3)
-        own[...] = term(z)
+        own[...] = term(3, z)
 
     def ring_mid(key, s2, r1, r2, hold):
         st["r2", key] = []
@@ -188,7 +213,7 @@
         st["g", k, h] = send(gbuf.at[k, h, 1 - core], gall.at[k, core, h], sib)
         gall[k, core, h] = gbuf[k, h, core]
 
-    numbers = {"Z": 0, "Y": 0}
+    numbers = {"Z": 0, "B": 0}
     index = {}
     for k in range(4):
         for h in range(2):
@@ -199,7 +224,7 @@
         n = index[k, h]
         ready(k, h)
 
-        def term(zb):
+        def term(i, zb):
             return jnp.dot(hs[pl.ds(2 * zb, 2)].reshape(480, 1024), cs[k, h], preferred_element_type=f32)
 
         ring_start(("z", n), term, zs1.at[n], zsb.at[n], zr1.at[n], zrb.at[n], zhold.at[n], zown.at[n])
@@ -224,25 +249,33 @@
         total = zown[n, mine, :] + zyr[n].astype(f32)
         finish(k, h, total[:, :128], total[:, 128:])
 
-    def yc(k, h):
+    def bs(k, h):
         n = index[k, h]
         ready(k, h)
-        for i in range(4):
-            hidden(i)
-
-        def body(zb, carry):
-            yys[n, zb] = jnp.dot(hs[2 * zb + 1 - y_lo], cs[k, h], preferred_element_type=f32).astype(bf16)
-            return carry
-
-        lax.fori_loop(0, 4, body, 0)
-        st["yy", n] = send(yys.at[n], yyr.at[n], across)
-
-    def ys(k, h):
-        n = index[k, h]
-        st["yy", n].wait_recv()
-
-        def term(zb):
-            return jnp.dot(hs[2 * zb + y_lo], cs[k, h], preferred_element_type=f32) + yyr[n, zb].astype(f32)
+        base = (x % 2) * 512
+        near = pl.ds(pl.multiple_of(base, 16), NEAR)
+        rest = pl.ds(pl.multiple_of(base + NEAR, 16), 512 - NEAR)
+        st["by", n] = [send(cs.at[k, h, near], co.at[n, near], across), send(cs.at[k, h, rest], co.at[n, rest], other)]
+
+    def bf(k, h):
+        n = index[k, h]
+        for copy in st["by", n]:
+            copy.wait_recv()
+        base = (x % 2) * 512
+        low, high = pl.ds(pl.multiple_of(base, 16), 256), pl.ds(pl.multiple_of(base + 256, 16), 256)
+        st["bx", n] = [send(co.at[n, low], co.at[n, low], x_up), send(co.at[n, high], co.at[n, high], x_down)]
+
+    def bz(k, h):
+        n = index[k, h]
+        for copy in st["bx", n]:
+            copy.wait_recv()
+
+        def term(i, zb):
+            if ("far", i) not in st:
+                st["far", i] = True
+                st["hs", i].wait_recv()
+            return (jnp.dot(hs[2 * zb + y_lo], cs[k, h], preferred_element_type=f32)
+                    + jnp.dot(ho[i], co[n], preferred_element_type=f32))
 
         ring_start(("y", n), term, ys1.at[n], ysb.at[n], yr1.at[n], yrb.at[n], yhold.at[n], yown.at[n])
 
@@ -311,7 +344,7 @@
         for copy in st["s", k]:
             copy.wait_recv()
         if "swap" not in st:
-            swap.wait_recv()
+            st["sw"].wait_recv()
             st["swap"] = True
         lhs = abuf[...].reshape(384, 1024)
 
@@ -399,7 +432,7 @@
 
         lax.fori_loop(0, 2, rows, 0)
 
-    steps = {"zc": zc, "zm": zm_, "ze": ze, "zf": zf_, "yc": yc, "ys": ys, "ym": ym, "ye": ye, "ad": ad,
+    steps = {"zc": zc, "zm": zm_, "ze": ze, "zf": zf_, "hf": hf, "bs": bs, "bf": bf, "bz": bz, "ac": ac, "sw": sw, "ym": ym, "ye": ye, "ad": ad,
              "ga": ga, "gb": gb, "gc": gc, "mm": mm, "f2": f2, "f3": f3, "f5": f5, "ap": ap, "at": at}
     for name, *where in ORDER:
         steps[name](*where)
@@ -408,14 +441,13 @@
 
 
 def fused(learn_hidden, out_cot, acts, queries, keys, values, keys_new, values_new, lengths, residual, master, first, second):
-    ht = learn_hidden.T.reshape(8, 240, 512)
     kinds = [a for pair in KIND for a in pair]
-    nz, ny = max(kinds.count("Z"), 1), max(kinds.count("Y"), 1)
+    nz, ny = max(kinds.count("Z"), 1), max(kinds.count("B"), 1)
 
     def ring(n, r):
         return [pltpu.VMEM((n, 2, r, 128), bf16)] * 7 + [pltpu.VMEM((n, r, 256), f32)]
 
-    copies = 4 + 16 + 1 + 8 * 8 + 4 * 24
+    copies = 12 + 16 + 1 + 8 * 10 + 4 * 24
     locals_ = 4 + 16 + 2 + 4 * (24 + 1)
     return pl.pallas_call(
         fused_kernel,
@@ -431,8 +463,9 @@
             *ring(nz, 480),
             pltpu.VMEM((nz, 240, 256), bf16),
             pltpu.VMEM((nz, 240, 256), bf16),
-            pltpu.VMEM((ny, 4, 240, 256), bf16),
-            pltpu.VMEM((ny, 4, 240, 256), bf16),
+            pltpu.VMEM((512, 1920), bf16),
+            pltpu.VMEM((4, 240, 1024), bf16),
+            pltpu.VMEM((ny, 1024, 256), bf16),
             *ring(ny, 240),
             pltpu.VMEM((4, 2, 2, 120, 256), f32),
             pltpu.VMEM((4, 2, 2, 120, 256), f32),
@@ -457,7 +490,7 @@
         compiler_params=pltpu.CompilerParams(collective_id=0, has_side_effects=True, vmem_limit_bytes=60 * 2**20),
         cost_estimate=pl.CostEstimate(flops=11274289152, bytes_accessed=20 * 2**20, transcendentals=0),
         name="fused",
-    )(ht, out_cot, acts, queries, keys, values, keys_new, values_new, lengths, residual, master, first, second)
+    )(learn_hidden, out_cot, acts, queries, keys, values, keys_new, values_new, lengths, residual, master, first, second)
 
 
 def local(

time: 148 us -> 133 us (0.90)
  Pallas kernels: 136 us -> 126 us
  local copies, waits for them, and re-layouts: 4.67 us -> 0.69 us
    pallas_call x1, Pallas kernels: 136 us -> 126 us  [fused(): pl.pallas_call(fused_kernel, out_shape=(jax.ShapeDtypeStruct((192, 512),...]
    transpose x1 -> x0, local copies, waits for them, and re-layouts: 3.98 us -> none  [fused(): ht = learn_hidden.T.reshape(8, 240, 512)]
where the time goes in v5:
time: 133 us
  Pallas kernels  126 us (95%)
  other arithmetic  5.84 us (4%)
    pallas_call x1, Pallas kernels, fused(): pl.pallas_call(fused_kernel, out_shape=(jax.ShapeDtypeStruct((192, 512),...  126 us
    sub x1, other arithmetic, local(): master - learn_rate * (first_hat / (jnp.sqrt(second_hat) + adam_eps) + de...  5.84 us

profile of v5, /device:TPU:0, one launch (start us, length us, event | category | flops | bytes accessed | tf_op | source)
XLA Modules:
  0.0 133.1 jit_solution(4968984739148116110)
XLA Ops:
  0.6 0.0 copy-start
  0.6 0.0 copy-start.1
  0.7 125.8 %fused.1 = (bf16[192,512]{1,0:T(8,128)(2,1)}, f32[120,4096]{1,0:T(8,128)}) custom-call(bf16[512,1920]{1,0:T(8,128)(2,1)} %hidden_in.1, bf16[512,4096]{1,0:T(8,128)(2,1)} %cot.1, bf16[192,1920]{1,0:T(8,128)(2,1)} %bitcast.4, bf16[4,48,512]{2,1,0:T(8,128)(2,1)} %queries.1, bf16[48,128,128]{2,1,0:T(8,128)(2,1)} %keys.1, bf16[48,128,128]{2,1,0:T(8,128)(2,1)} %values.1, ...), custom_call_target="tpu_custom_call" | custom-call | flops 11274289152 | bytes 20971520 | tf_op jit(solution)/shard_map/fused/pallas_call | solution.py:452
  126.5 0.0 copy-done
  126.5 0.0 copy-done.1
  126.5 0.0 copy-start.2
  126.5 5.8 %multiply_subtract_fusion = (f32[120,4096]{1,0:T(8,128)}, f32[120,4096]{1,0:T(8,128)}, f32[120,4096]{1,0:T(8,128)}) fusion(f32[120,4096]{1,0:T(8,128)S(1)} %copy-done, f32[120,4096]{1,0:T(8,128)} %get-tuple-element.7, f32[120,4096]{1,0:T(8,128)S(1)} %copy-done.1, f32[120,4096]{1,0:T(8,128)} %second.1), kind=kLoop, calls=%fused_computation.2 | loop fusion | flops 7372800 | bytes 13762560 | tf_op jit(solution)/shard_map/sub | solution.py:520
  132.4 0.0 copy-done.2
  132.4 0.7 copy.18
Async XLA Ops:
  0.6 125.9 %copy-start = (f32[120,4096]{1,0:T(8,128)S(1)}, f32[120,4096]{1,0:T(8,128)}, u32[]{:S(2)}) copy-start(f32[120,4096]{1,0:T(8,128)} %master.1) | copy-start | bytes 5898244
  0.6 125.9 %copy-start.1 = (f32[120,4096]{1,0:T(8,128)S(1)}, f32[120,4096]{1,0:T(8,128)}, u32[]{:S(2)}) copy-start(f32[120,4096]{1,0:T(8,128)} %first.1) | copy-start | bytes 5898244
  126.5 5.9 %copy-start.2 = (bf16[192,512]{1,0:T(8,128)(2,1)S(1)}, bf16[192,512]{1,0:T(8,128)(2,1)}, u32[]{:S(2)}) copy-start(bf16[192,512]{1,0:T(8,128)(2,1)} %get-tuple-element.6) | copy-start | bytes 589828

commit v6 on v5

--- a/solution.py
+++ b/solution.py
@@ -13,18 +13,20 @@
 HEAD_DIM = 128
 CHUNKS = 4
 KIND = (("Z", "Z"), ("Z", "B"), ("B", "B"), ("B", "B"))
-NEAR = 192
+NEAR = (0, 0, 192, 256, 320)
 ORDER = [
-    ("zc", 0, 1), ("bs", 1, 1), ("bs", 2, 0), ("zc", 1, 0), ("bs", 2, 1), ("hf", 0), ("bs", 3, 1), ("zm", 0, 1),
-    ("ac",), ("ap",), ("zm", 1, 0), ("zc", 0, 0), ("ze", 0, 1), ("bf", 1, 1), ("hf", 1), ("hf", 2), ("hf", 3),
-    ("zm", 0, 0), ("bf", 2, 0), ("at", 0), ("bz", 1, 1), ("bf", 2, 1), ("bf", 3, 1), ("bs", 3, 0), ("bz", 2, 0),
-    ("ze", 0, 0), ("zf", 0, 1), ("ym", 1, 1), ("bz", 2, 1), ("ym", 2, 0), ("bf", 3, 0), ("ze", 1, 0), ("zf", 0, 0),
-    ("bz", 3, 1), ("ad", 0), ("ym", 2, 1), ("bz", 3, 0), ("ye", 2, 0), ("ye", 1, 1), ("zf", 1, 0), ("ga", 0),
-    ("at", 1), ("ym", 3, 1), ("ye", 2, 1), ("ad", 1), ("ad", 2), ("ym", 3, 0), ("sw",), ("gb", 0), ("ga", 1),
-    ("ye", 3, 0), ("gc", 0), ("at", 2), ("ye", 3, 1), ("ga", 2), ("ad", 3), ("gb", 1), ("at", 3), ("mm", 0),
-    ("gb", 2), ("f2", 0), ("ga", 3), ("gc", 1), ("mm", 1), ("gc", 2), ("mm", 2), ("f2", 1), ("gb", 3), ("f2", 2),
-    ("gc", 3), ("at", 4), ("mm", 3), ("f3", 0), ("at", 5), ("f3", 1), ("f3", 2), ("f5", 0), ("f2", 3), ("f5", 1),
-    ("f3", 3), ("f5", 2), ("f5", 3),
+    ("za", 0, 0), ("bs", 1, 1), ("ap",), ("za", 1, 0), ("za", 0, 1), ("zb", 0, 0), ("zm", 0, 0), ("zb", 1, 0),
+    ("hf", 0), ("bs", 2, 0), ("zc", 0, 0), ("at", 0), ("bs", 2, 1), ("bf", 1, 1), ("at", 1), ("hf", 1), ("bs", 3, 1),
+    ("hf", 2), ("bf", 2, 0), ("zb", 0, 1), ("zm", 1, 0), ("at", 2), ("zc", 0, 1), ("ya", 2, 0), ("ya", 1, 1),
+    ("hf", 3), ("ac",), ("zm", 0, 1), ("bs", 3, 0), ("bf", 2, 1), ("yb", 1, 1), ("yb", 2, 0), ("ze", 0, 0),
+    ("bf", 3, 1), ("ym", 1, 1), ("zc", 1, 0), ("ze", 0, 1), ("ya", 2, 1), ("bf", 3, 0), ("ze", 1, 0), ("ya", 3, 1),
+    ("yc", 2, 0), ("yb", 2, 1), ("ym", 2, 0), ("yc", 1, 1), ("yb", 3, 1), ("ya", 3, 0), ("zf", 0, 0), ("zf", 0, 1),
+    ("ym", 2, 1), ("ye", 1, 1), ("yb", 3, 0), ("ad", 0), ("yc", 2, 1), ("zf", 1, 0), ("ym", 3, 1), ("yc", 3, 1),
+    ("ym", 3, 0), ("ad", 1), ("ga", 0), ("ye", 2, 1), ("yc", 3, 0), ("ye", 2, 0), ("ye", 3, 0), ("sw",), ("ad", 2),
+    ("ga", 1), ("at", 3), ("ye", 3, 1), ("gb", 0), ("ad", 3), ("gb", 1), ("gc", 0), ("ga", 2), ("gc", 1), ("mm", 0),
+    ("mm", 1), ("ga", 3), ("f2", 0), ("gb", 2), ("f2", 1), ("at", 4), ("gb", 3), ("at", 5), ("f3", 0), ("gc", 2),
+    ("f3", 1), ("gc", 3), ("mm", 2), ("mm", 3), ("f2", 2), ("f2", 3), ("f5", 1), ("f5", 0), ("f3", 2), ("f3", 3),
+    ("f5", 2), ("f5", 3),
 ]
 beta_one = 0.9
 beta_two = 0.999
@@ -46,7 +48,7 @@
 def fused_kernel(hidden_in, cot, acts, queries, keys, values, keys_new, values_new, lengths, residual,
                  master, first, second, out, grad,
                  hs, cs, zs1, zsb, zs2, zr1, zrb, zr2, zhold, zown, zys, zyr,
-                 hraw, ho, co, ys1, ysb, ys2, yr1, yrb, yr2, yhold, yown, gbuf, gall, adam,
+                 hraw, ho, co, ys1, ysb, ys2, yr1, yrb, yr2, yhold, yown, gbuf, adam,
                  wsend, wbuf, asend, abuf, part, r1, rb, s2, r2, q, ug, kbuf, vbuf, qbuf, nbuf, att,
                  loc_sem, send_sem, recv_sem):
     z, y_lo, core, x, y_hi = coords()
@@ -57,8 +59,9 @@
 
     sib = place(z, y_lo, 1 - core, x, y_hi)
     z_up, z_down = place((z + 1) % 4, y_lo, core, x, y_hi), place((z + 3) % 4, y_lo, core, x, y_hi)
-    x_up, x_down = place(z, y_lo, core, (x + 1) % 4, y_hi), place(z, y_lo, core, (x + 3) % 4, y_hi)
     y_place = [at_y((y + d) % 4) for d in range(1, 4)]
+    x_place = [place(z, y_lo, core, (x + d) % 4, y_hi) for d in range(1, 4)]
+    axes = ((x, x_place[0], x_place[2]), (y, y_place[0], y_place[2]))
     across = place(z, 1 - y_lo, core, x, y_hi)
     peers = [((x + i // 2) % 4, (y_hi + i % 2) % 2) for i in range(1, 8)]
     peer_place = [place(z, y_lo, core, px, py) for px, py in peers]
@@ -123,7 +126,7 @@
             st["c", k, h].append(send(cot.at[:, theirs], cs.at[k, h, pl.ds(512, 512), lanes], sib))
             st["c", k, h].append(local(cot.at[:, mine], cs.at[k, h, pl.ds(0, 512), lanes]))
 
-    first_use = [where for name, *where in ORDER if name in ("bs", "zc")]
+    first_use = [where for name, *where in ORDER if name in ("bs", "za")]
     raw.wait()
     turn_hidden(0)
     pl.semaphore_wait(barrier, len(everyone))
@@ -134,7 +137,12 @@
         share_hidden(i)
     for where in first_use[1:]:
         share_cotangent(*where)
-    st["kv"] = [local(keys, kbuf), local(values, vbuf)]
+
+    def cache_fetch(i):
+        rows = pl.ds(i * 8, 8)
+        st["kv", i] = [local(keys.at[rows], kbuf.at[i % 2]), local(values.at[rows], vbuf.at[i % 2])]
+
+    cache_fetch(0)
 
     def hidden(i):
         if ("got", i) not in st:
@@ -171,12 +179,14 @@
             st["c", k, h][2 * i].wait_recv()
             st["c", k, h][2 * i + 1].wait()
 
-    def ring_start(key, term, s1, sb, r1, rb, hold, own):
+    def ring_a(key, term, s1, r1):
         hidden(0)
         p = term(0, zf)
         s1[0] = p[:, :128].astype(bf16)
         s1[1] = p[:, 128:].astype(bf16)
         st["r1", key] = [send(s1.at[0], r1.at[0], z_up), send(s1.at[1], r1.at[1], z_down)]
+
+    def ring_b(key, term, sb, rb, hold):
         hidden(1)
         p = term(1, zp)
         sb[0] = p[:, 128:].astype(bf16)
@@ -188,6 +198,8 @@
         b1 = send(sb.at[1], rb.at[1], z_down)
         hold[1] = p[:, 128:].astype(hold.dtype)
         st["rb", key] = [b0, b1]
+
+    def ring_c(term, own):
         hidden(3)
         own[...] = term(3, z)
 
@@ -208,10 +220,15 @@
         return left, right
 
     def finish(k, h, left, right):
-        gbuf[k, h, :, :, pl.ds(0, 128)] = left.reshape(2, 120, 128)
-        gbuf[k, h, :, :, pl.ds(128, 128)] = right.reshape(2, 120, 128)
-        st["g", k, h] = send(gbuf.at[k, h, 1 - core], gall.at[k, core, h], sib)
-        gall[k, core, h] = gbuf[k, h, core]
+        for copy in st.get(("g", k - 2, h), []):
+            copy.wait_send()
+            sends[:] = [c for c in sends if c is not copy]
+        st["g", k, h] = []
+        for i, half in enumerate((left, right)):
+            gbuf[k % 2, h, i] = half.reshape(2, 120, 128)
+            cols = pl.ds(pl.multiple_of((4 * core + 2 * h + i) * 512 + k * 128, 128), 128)
+            st["g", k, h].append(send(gbuf.at[k % 2, h, i, 1 - core], grad.at[:, cols], sib))
+            grad[:, cols] = gbuf[k % 2, h, i, core]
 
     numbers = {"Z": 0, "B": 0}
     index = {}
@@ -220,14 +237,23 @@
             index[k, h] = numbers[KIND[k][h]]
             numbers[KIND[k][h]] += 1
 
-    def zc(k, h):
-        n = index[k, h]
-        ready(k, h)
-
+    def zterm(k, h):
         def term(i, zb):
             return jnp.dot(hs[pl.ds(2 * zb, 2)].reshape(480, 1024), cs[k, h], preferred_element_type=f32)
 
-        ring_start(("z", n), term, zs1.at[n], zsb.at[n], zr1.at[n], zrb.at[n], zhold.at[n], zown.at[n])
+        return term
+
+    def za(k, h):
+        n = index[k, h]
+        ready(k, h)
+        ring_a(("z", n), zterm(k, h), zs1.at[n], zr1.at[n])
+
+    def zb_(k, h):
+        n = index[k, h]
+        ring_b(("z", n), zterm(k, h), zsb.at[n], zrb.at[n], zhold.at[n])
+
+    def zc(k, h):
+        ring_c(zterm(k, h), zown.at[index[k, h]])
 
     def zm_(k, h):
         n = index[k, h]
@@ -253,9 +279,12 @@
         n = index[k, h]
         ready(k, h)
         base = (x % 2) * 512
-        near = pl.ds(pl.multiple_of(base, 16), NEAR)
-        rest = pl.ds(pl.multiple_of(base + NEAR, 16), 512 - NEAR)
-        st["by", n] = [send(cs.at[k, h, near], co.at[n, near], across), send(cs.at[k, h, rest], co.at[n, rest], other)]
+        few = NEAR[n]
+        rest = pl.ds(pl.multiple_of(base + few, 16), 512 - few)
+        st["by", n] = [send(cs.at[k, h, rest], co.at[n, rest], other)]
+        if few > 0:
+            near = pl.ds(pl.multiple_of(base, 16), few)
+            st["by", n].append(send(cs.at[k, h, near], co.at[n, near], across))
 
     def bf(k, h):
         n = index[k, h]
@@ -263,12 +292,10 @@
             copy.wait_recv()
         base = (x % 2) * 512
         low, high = pl.ds(pl.multiple_of(base, 16), 256), pl.ds(pl.multiple_of(base + 256, 16), 256)
-        st["bx", n] = [send(co.at[n, low], co.at[n, low], x_up), send(co.at[n, high], co.at[n, high], x_down)]
-
-    def bz(k, h):
-        n = index[k, h]
-        for copy in st["bx", n]:
-            copy.wait_recv()
+        st["bx", n] = [send(co.at[n, low], co.at[n, low], x_place[0]), send(co.at[n, high], co.at[n, high], x_place[2])]
+
+    def bterm(k, h):
+        n = index[k, h]
 
         def term(i, zb):
             if ("far", i) not in st:
@@ -277,7 +304,20 @@
             return (jnp.dot(hs[2 * zb + y_lo], cs[k, h], preferred_element_type=f32)
                     + jnp.dot(ho[i], co[n], preferred_element_type=f32))
 
-        ring_start(("y", n), term, ys1.at[n], ysb.at[n], yr1.at[n], yrb.at[n], yhold.at[n], yown.at[n])
+        return term
+
+    def ya(k, h):
+        n = index[k, h]
+        for copy in st["bx", n]:
+            copy.wait_recv()
+        ring_a(("y", n), bterm(k, h), ys1.at[n], yr1.at[n])
+
+    def yb(k, h):
+        n = index[k, h]
+        ring_b(("y", n), bterm(k, h), ysb.at[n], yrb.at[n], yhold.at[n])
+
+    def yc(k, h):
+        ring_c(bterm(k, h), yown.at[index[k, h]])
 
     def ym(k, h):
         n = index[k, h]
@@ -290,7 +330,8 @@
 
     def ad(k):
         for h in range(2):
-            st["g", k, h].wait_recv()
+            for copy in st["g", k, h]:
+                copy.wait_recv()
         if k < 3:
             adam_fetch(k + 1)
         row = lax.broadcasted_iota(jnp.int32, (128, 120), 0)
@@ -299,8 +340,7 @@
         for b in range(8):
             for i in range(3):
                 st["m", k, b, i].wait()
-            g = gall[k, b // 4, (b // 2) % 2, :, (b % 2) * 128:(b % 2 + 1) * 128]
-            grad[:, b * 512 + k * 128:b * 512 + (k + 1) * 128] = g
+            g = grad[:, b * 512 + k * 128:b * 512 + (k + 1) * 128]
             m = adam[k % 2, 0, b]
             one = beta_one * adam[k % 2, 1, b] + (1.0 - beta_one) * g
             two = beta_two * adam[k % 2, 2, b] + (1.0 - beta_two) * g * g
@@ -353,52 +393,66 @@
             rhs = wbuf[k, :, :, :, cols].reshape(1024, 256)
             p = jnp.dot(lhs, rhs, preferred_element_type=f32).astype(bf16)
             for i in range(4):
-                part[k, n, i] = p[(i % 2) * 192:(i % 2 + 1) * 192, (i // 2) * 128:(i // 2 + 1) * 128]
+                piece = p[(i % 2) * 192:(i % 2 + 1) * 192, (i // 2) * 128:(i // 2 + 1) * 128]
+                part[k, 0, n, i] = piece[:96]
+                part[k, 1, i, n] = piece[96:]
             return carry
 
         lax.fori_loop(0, 4, body, 0)
-        far, above, below = (x + 2) % 4, (x + 1) % 4, (x + 3) % 4
         lo, hi = pl.ds(0, 2), pl.ds(2, 2)
-        st["f1", k] = [send(part.at[k, far, lo], r1.at[k, 0], x_up), send(part.at[k, far, hi], r1.at[k, 1], x_down)]
-        st["fb", k] = [send(part.at[k, above, hi], rb.at[k, 0], x_up), send(part.at[k, below, lo], rb.at[k, 1], x_down)]
+        for d, (me, up, down) in enumerate(axes):
+            far, above, below = (me + 2) % 4, (me + 1) % 4, (me + 3) % 4
+            st["f1", k, d] = [send(part.at[k, d, far, lo], r1.at[k, d, 0], up),
+                              send(part.at[k, d, far, hi], r1.at[k, d, 1], down)]
+            st["fb", k, d] = [send(part.at[k, d, above, hi], rb.at[k, d, 0], up),
+                              send(part.at[k, d, below, lo], rb.at[k, d, 1], down)]
 
     def f2(k):
-        above, below = (x + 1) % 4, (x + 3) % 4
-        st["f1", k][0].wait_recv()
-        s2[k, 0] = (part[k, above, pl.ds(0, 2)].astype(f32) + r1[k, 0].astype(f32)).astype(bf16)
-        a = send(s2.at[k, 0], r2.at[k, 0], x_up)
-        st["f1", k][1].wait_recv()
-        s2[k, 1] = (part[k, below, pl.ds(2, 2)].astype(f32) + r1[k, 1].astype(f32)).astype(bf16)
-        st["f2", k] = [a, send(s2.at[k, 1], r2.at[k, 1], x_down)]
+        for d, (me, up, down) in enumerate(axes):
+            above, below = (me + 1) % 4, (me + 3) % 4
+            st["f1", k, d][0].wait_recv()
+            s2[k, d, 0] = (part[k, d, above, pl.ds(0, 2)].astype(f32) + r1[k, d, 0].astype(f32)).astype(bf16)
+            first_half = send(s2.at[k, d, 0], r2.at[k, d, 0], up)
+            st["f1", k, d][1].wait_recv()
+            s2[k, d, 1] = (part[k, d, below, pl.ds(2, 2)].astype(f32) + r1[k, d, 1].astype(f32)).astype(bf16)
+            st["f2", k, d] = [first_half, send(s2.at[k, d, 1], r2.at[k, d, 1], down)]
 
     def f3(k):
-        st["fb", k][1].wait_recv()
-        st["f2", k][0].wait_recv()
-        q[k, pl.ds(0, 2)] = (part[k, x, pl.ds(0, 2)].astype(f32) + rb[k, 1].astype(f32) + r2[k, 0].astype(f32)).astype(bf16)
-        st["fb", k][0].wait_recv()
-        st["f2", k][1].wait_recv()
-        q[k, pl.ds(2, 2)] = (part[k, x, pl.ds(2, 2)].astype(f32) + rb[k, 0].astype(f32) + r2[k, 1].astype(f32)).astype(bf16)
-        st["g", k] = [send(q.at[k, (y + d) % 4], ug.at[k, d - 1], y_place[d - 1]) for d in range(1, 4)]
+        for d, (me, up, down) in enumerate(axes):
+            st["fb", k, d][1].wait_recv()
+            st["f2", k, d][0].wait_recv()
+            q[k, d, pl.ds(0, 2)] = (part[k, d, me, pl.ds(0, 2)].astype(f32) + rb[k, d, 1].astype(f32)
+                                    + r2[k, d, 0].astype(f32)).astype(bf16)
+            st["fb", k, d][0].wait_recv()
+            st["f2", k, d][1].wait_recv()
+            q[k, d, pl.ds(2, 2)] = (part[k, d, me, pl.ds(2, 2)].astype(f32) + rb[k, d, 0].astype(f32)
+                                    + r2[k, d, 1].astype(f32)).astype(bf16)
+            along, devices = (y, y_place) if d == 0 else (x, x_place)
+            st["g", k, d] = [send(q.at[k, d, (along + i) % 4], ug.at[k, d, i - 1], devices[i - 1]) for i in range(1, 4)]
 
     def f5(k):
         cols = pl.ds(k * 128, 128)
-        total = q[k, y].astype(f32)
-        for i in range(3):
-            st["g", k][i].wait_recv()
-            total = total + ug[k, i].astype(f32)
-        attended = att[:, k].reshape(192, 128).astype(bf16).astype(f32)
-        stream = (residual[:, cols].astype(f32) + attended).astype(bf16)
-        out[:, cols] = (stream.astype(f32) + total).astype(bf16)
+        for d in range(2):
+            lines = pl.ds(d * 96, 96)
+            total = q[k, d, y if d == 0 else x].astype(f32)
+            for i in range(3):
+                st["g", k, d][i].wait_recv()
+                total = total + ug[k, d, i].astype(f32)
+            attended = att[pl.ds(2 * d, 2), k].reshape(96, 128).astype(bf16).astype(f32)
+            stream = (residual[lines, cols].astype(f32) + attended).astype(bf16)
+            out[lines, cols] = (stream.astype(f32) + total).astype(bf16)
 
     def ap():
         for g in range(HEADS // KV_HEADS):
             qbuf[:, g] = queries[:, :, g * 128:(g + 1) * 128].astype(f32)
         nbuf[0] = keys_new[...].astype(f32)
         nbuf[1] = values_new[...].astype(f32)
-        for copy in st["kv"]:
+
+    def at(i):
+        for copy in st["kv", i]:
             copy.wait()
-
-    def at(i):
+        if i < 5:
+            cache_fetch(i + 1)
         position = lax.broadcasted_iota(jnp.int32, (16, 128), 1)
         when = lax.broadcasted_iota(jnp.int32, (16, 1), 0) // 4
         heads = HEADS // KV_HEADS
@@ -408,7 +462,7 @@
                 r = i * 8 + n * 4 + j
                 qr = jnp.concatenate(
                     [qbuf[t, g, pl.ds(r, 1), :] for t in range(4) for g in range(heads)], axis=0)
-                cached = lax.dot_general(qr.astype(bf16), kbuf[r], (((1,), (1,)), ((), ())),
+                cached = lax.dot_general(qr.astype(bf16), kbuf[i % 2, n * 4 + j], (((1,), (1,)), ((), ())),
                                          preferred_element_type=f32) * HEAD_DIM ** (-0.5)
                 cached = jnp.where(position < lengths[r], cached, -jnp.inf)
                 fresh = []
@@ -421,7 +475,7 @@
                 cached = jnp.exp(cached - highest)
                 fresh = [jnp.exp(score - highest) for score in fresh]
                 total = jnp.sum(cached, axis=1, keepdims=True) + (fresh[0] + fresh[1]) + (fresh[2] + fresh[3])
-                result = jnp.dot((cached / total).astype(bf16), vbuf[r], preferred_element_type=f32)
+                result = jnp.dot((cached / total).astype(bf16), vbuf[i % 2, n * 4 + j], preferred_element_type=f32)
                 for s in range(4):
                     weight = (fresh[s] / total).astype(bf16).astype(f32)
                     result = result + weight * nbuf[1, s, pl.ds(r, 1), :]
@@ -432,8 +486,9 @@
 
         lax.fori_loop(0, 2, rows, 0)
 
-    steps = {"zc": zc, "zm": zm_, "ze": ze, "zf": zf_, "hf": hf, "bs": bs, "bf": bf, "bz": bz, "ac": ac, "sw": sw, "ym": ym, "ye": ye, "ad": ad,
-             "ga": ga, "gb": gb, "gc": gc, "mm": mm, "f2": f2, "f3": f3, "f5": f5, "ap": ap, "at": at}
+    steps = {"za": za, "zb": zb_, "zc": zc, "zm": zm_, "ze": ze, "zf": zf_, "hf": hf, "bs": bs, "bf": bf, "ya": ya,
+             "yb": yb, "yc": yc, "ym": ym, "ye": ye, "ad": ad, "ga": ga, "gb": gb, "gc": gc, "mm": mm, "f2": f2,
+             "f3": f3, "f5": f5, "ac": ac, "sw": sw, "ap": ap, "at": at}
     for name, *where in ORDER:
         steps[name](*where)
     for copy in sends:
@@ -447,8 +502,8 @@
     def ring(n, r):
         return [pltpu.VMEM((n, 2, r, 128), bf16)] * 7 + [pltpu.VMEM((n, r, 256), f32)]
 
-    copies = 12 + 16 + 1 + 8 * 10 + 4 * 24
-    locals_ = 4 + 16 + 2 + 4 * (24 + 1)
+    copies = 12 + 16 + 1 + 8 * 11 + 4 * 33
+    locals_ = 4 + 16 + 12 + 4 * (24 + 1)
     return pl.pallas_call(
         fused_kernel,
         out_shape=(jax.ShapeDtypeStruct((192, 512), bf16), jax.ShapeDtypeStruct((120, 4096), f32)),
@@ -467,19 +522,18 @@
             pltpu.VMEM((4, 240, 1024), bf16),
             pltpu.VMEM((ny, 1024, 256), bf16),
             *ring(ny, 240),
-            pltpu.VMEM((4, 2, 2, 120, 256), f32),
-            pltpu.VMEM((4, 2, 2, 120, 256), f32),
+            pltpu.VMEM((2, 2, 2, 2, 120, 128), f32),
             pltpu.VMEM((2, 3, 8, 120, 128), f32),
             pltpu.VMEM((4, 8, 16, 1024), bf16),
             pltpu.VMEM((4, 8, 8, 16, 1024), bf16),
             pltpu.VMEM((2, 192, 1024), bf16),
             pltpu.VMEM((2, 192, 1024), bf16),
-            pltpu.VMEM((4, 4, 4, 192, 128), bf16),
-            *[pltpu.VMEM((4, 2, 2, 192, 128), bf16)] * 4,
-            pltpu.VMEM((4, 4, 192, 128), bf16),
-            pltpu.VMEM((4, 3, 192, 128), bf16),
-            pltpu.VMEM((48, 128, 128), bf16),
-            pltpu.VMEM((48, 128, 128), bf16),
+            pltpu.VMEM((4, 2, 4, 4, 96, 128), bf16),
+            *[pltpu.VMEM((4, 2, 2, 2, 96, 128), bf16)] * 4,
+            pltpu.VMEM((4, 2, 4, 96, 128), bf16),
+            pltpu.VMEM((4, 2, 3, 96, 128), bf16),
+            pltpu.VMEM((2, 8, 128, 128), bf16),
+            pltpu.VMEM((2, 8, 128, 128), bf16),
             pltpu.VMEM((4, 4, 48, 128), f32),
             pltpu.VMEM((2, 4, 48, 128), f32),
             pltpu.VMEM((4, 4, 48, 128), f32),
@@ -487,7 +541,7 @@
             pltpu.SemaphoreType.DMA((copies,)),
             pltpu.SemaphoreType.DMA((copies,)),
         ],
-        compiler_params=pltpu.CompilerParams(collective_id=0, has_side_effects=True, vmem_limit_bytes=60 * 2**20),
+        compiler_params=pltpu.CompilerParams(collective_id=0, has_side_effects=True, vmem_limit_bytes=54 * 2**20),
         cost_estimate=pl.CostEstimate(flops=11274289152, bytes_accessed=20 * 2**20, transcendentals=0),
         name="fused",
     )(learn_hidden, out_cot, acts, queries, keys, values, keys_new, values_new, lengths, residual, master, first, second)

time: 133 us -> 125 us (0.940)
  Pallas kernels: 126 us -> 118 us
    pallas_call x1, Pallas kernels: 126 us -> 118 us  [fused(): pl.pallas_call(fused_kernel, out_shape=(jax.ShapeDtypeStruct((192, 512),...]
where the time goes in v6:
time: 125 us
  Pallas kernels  118 us (94%)
  other arithmetic  5.25 us (4%)
    pallas_call x1, Pallas kernels, fused(): pl.pallas_call(fused_kernel, out_shape=(jax.ShapeDtypeStruct((192, 512),...  118 us
    sub x1, other arithmetic, local(): master - learn_rate * (first_hat / (jnp.sqrt(second_hat) + adam_eps) + de...  5.25 us

profile of v6, /device:TPU:0, one launch (start us, length us, event | category | flops | bytes accessed | tf_op | source)
XLA Modules:
  0.0 124.7 jit_solution(6529085092746821660)
XLA Ops:
  0.6 0.0 copy-start
  0.6 0.0 copy-start.1
  0.7 0.0 copy-start.2
  0.7 118.0 %fused.1 = (bf16[192,512]{1,0:T(8,128)(2,1)}, f32[120,4096]{1,0:T(8,128)}) custom-call(bf16[512,1920]{1,0:T(8,128)(2,1)} %hidden_in.1, bf16[512,4096]{1,0:T(8,128)(2,1)} %cot.1, bf16[192,1920]{1,0:T(8,128)(2,1)} %bitcast.4, bf16[4,48,512]{2,1,0:T(8,128)(2,1)} %queries.1, bf16[48,128,128]{2,1,0:T(8,128)(2,1)} %keys.1, bf16[48,128,128]{2,1,0:T(8,128)(2,1)} %values.1, ...), custom_call_target="tpu_custom_call" | custom-call | flops 11274289152 | bytes 20971520 | tf_op jit(solution)/shard_map/fused/pallas_call | solution.py:507
  118.7 0.0 copy-done
  118.7 0.0 copy-done.1
  118.7 0.0 copy-done.2
  118.8 0.0 copy-start.3
  118.8 5.3 %multiply_subtract_fusion = (f32[120,4096]{1,0:T(8,128)}, f32[120,4096]{1,0:T(8,128)}, f32[120,4096]{1,0:T(8,128)}) fusion(f32[120,4096]{1,0:T(8,128)S(1)} %copy-done, f32[120,4096]{1,0:T(8,128)} %get-tuple-element.7, f32[120,4096]{1,0:T(8,128)S(1)} %copy-done.1, f32[120,4096]{1,0:T(8,128)S(1)} %copy-done.2), kind=kLoop, calls=%fused_computation.2 | loop fusion | flops 7372800 | bytes 13762560 | tf_op jit(solution)/shard_map/sub | solution.py:574
  124.0 0.0 copy-done.3
  124.0 0.7 copy.18
Async XLA Ops:
  0.6 118.1 %copy-start = (f32[120,4096]{1,0:T(8,128)S(1)}, f32[120,4096]{1,0:T(8,128)}, u32[]{:S(2)}) copy-start(f32[120,4096]{1,0:T(8,128)} %master.1) | copy-start | bytes 5898244
  0.6 118.1 %copy-start.1 = (f32[120,4096]{1,0:T(8,128)S(1)}, f32[120,4096]{1,0:T(8,128)}, u32[]{:S(2)}) copy-start(f32[120,4096]{1,0:T(8,128)} %first.1) | copy-start | bytes 5898244
  0.7 118.1 %copy-start.2 = (f32[120,4096]{1,0:T(8,128)S(1)}, f32[120,4096]{1,0:T(8,128)}, u32[]{:S(2)}) copy-start(f32[120,4096]{1,0:T(8,128)} %second.1) | copy-start | bytes 5898244
  118.8 5.3 %copy-start.3 = (bf16[192,512]{1,0:T(8,128)(2,1)S(1)}, bf16[192,512]{1,0:T(8,128)(2,1)}, u32[]{:S(2)}) copy-start(bf16[192,512]{1,0:T(8,128)(2,1)} %get-tuple-element.6) | copy-start | bytes 589828

commit v7 on v6

--- a/solution.py
+++ b/solution.py
@@ -12,21 +12,20 @@
 KV_HEADS = 8
 HEAD_DIM = 128
 CHUNKS = 4
-KIND = (("Z", "Z"), ("Z", "B"), ("B", "B"), ("B", "B"))
-NEAR = (0, 0, 192, 256, 320)
+KIND = (("Z", "B"), ("Z", "B"), ("B", "B"), ("B", "B"))
+NEAR = (0, 0, 64, 128, 256, 256)
 ORDER = [
-    ("za", 0, 0), ("bs", 1, 1), ("ap",), ("za", 1, 0), ("za", 0, 1), ("zb", 0, 0), ("zm", 0, 0), ("zb", 1, 0),
-    ("hf", 0), ("bs", 2, 0), ("zc", 0, 0), ("at", 0), ("bs", 2, 1), ("bf", 1, 1), ("at", 1), ("hf", 1), ("bs", 3, 1),
-    ("hf", 2), ("bf", 2, 0), ("zb", 0, 1), ("zm", 1, 0), ("at", 2), ("zc", 0, 1), ("ya", 2, 0), ("ya", 1, 1),
-    ("hf", 3), ("ac",), ("zm", 0, 1), ("bs", 3, 0), ("bf", 2, 1), ("yb", 1, 1), ("yb", 2, 0), ("ze", 0, 0),
-    ("bf", 3, 1), ("ym", 1, 1), ("zc", 1, 0), ("ze", 0, 1), ("ya", 2, 1), ("bf", 3, 0), ("ze", 1, 0), ("ya", 3, 1),
-    ("yc", 2, 0), ("yb", 2, 1), ("ym", 2, 0), ("yc", 1, 1), ("yb", 3, 1), ("ya", 3, 0), ("zf", 0, 0), ("zf", 0, 1),
-    ("ym", 2, 1), ("ye", 1, 1), ("yb", 3, 0), ("ad", 0), ("yc", 2, 1), ("zf", 1, 0), ("ym", 3, 1), ("yc", 3, 1),
-    ("ym", 3, 0), ("ad", 1), ("ga", 0), ("ye", 2, 1), ("yc", 3, 0), ("ye", 2, 0), ("ye", 3, 0), ("sw",), ("ad", 2),
-    ("ga", 1), ("at", 3), ("ye", 3, 1), ("gb", 0), ("ad", 3), ("gb", 1), ("gc", 0), ("ga", 2), ("gc", 1), ("mm", 0),
-    ("mm", 1), ("ga", 3), ("f2", 0), ("gb", 2), ("f2", 1), ("at", 4), ("gb", 3), ("at", 5), ("f3", 0), ("gc", 2),
-    ("f3", 1), ("gc", 3), ("mm", 2), ("mm", 3), ("f2", 2), ("f2", 3), ("f5", 1), ("f5", 0), ("f3", 2), ("f3", 3),
-    ("f5", 2), ("f5", 3),
+    ("bs", 1, 1), ("za", 1, 0), ("bs", 0, 1), ("zb", 1, 0), ("za", 0, 0), ("ac",), ("bs", 2, 0), ("bf", 1, 1),
+    ("zb", 0, 0), ("ap",), ("at", 0), ("hf", 0), ("zm", 0, 0), ("zc", 1, 0), ("zc", 0, 0), ("zm", 1, 0), ("bs", 2, 1),
+    ("bs", 3, 1), ("at", 1), ("bf", 0, 1), ("hf", 1), ("at", 2), ("at", 3), ("hf", 2), ("ya", 1, 1), ("ze", 0, 0),
+    ("ya", 0, 1), ("yb", 0, 1), ("bf", 2, 0), ("hf", 3), ("yb", 1, 1), ("ym", 0, 1), ("bs", 3, 0), ("bf", 2, 1),
+    ("yc", 1, 1), ("ze", 1, 0), ("ym", 1, 1), ("yc", 0, 1), ("ya", 2, 0), ("bf", 3, 1), ("yb", 2, 0), ("ya", 2, 1),
+    ("yb", 2, 1), ("zf", 0, 0), ("ye", 0, 1), ("yc", 2, 1), ("ym", 2, 0), ("bf", 3, 0), ("ya", 3, 1), ("ym", 2, 1),
+    ("yb", 3, 1), ("ad", 0), ("ya", 3, 0), ("yb", 3, 0), ("ye", 1, 1), ("ym", 3, 1), ("yc", 3, 1), ("yc", 2, 0),
+    ("zf", 1, 0), ("ga", 0), ("ye", 2, 0), ("ye", 2, 1), ("ad", 1), ("ad", 2), ("ye", 3, 1), ("yc", 3, 0),
+    ("ym", 3, 0), ("ga", 1), ("sw",), ("gb", 0), ("ye", 3, 0), ("at", 4), ("ga", 2), ("ad", 3), ("gc", 0), ("gb", 1),
+    ("mm", 0), ("at", 5), ("ga", 3), ("gc", 1), ("gb", 2), ("mm", 1), ("f3", 0), ("gb", 3), ("gc", 2), ("f3", 1),
+    ("mm", 2), ("gc", 3), ("f5", 0), ("mm", 3), ("f3", 2), ("f3", 3), ("f5", 2), ("f5", 1), ("f5", 3),
 ]
 beta_one = 0.9
 beta_two = 0.999
@@ -46,10 +45,10 @@
 
 
 def fused_kernel(hidden_in, cot, acts, queries, keys, values, keys_new, values_new, lengths, residual,
-                 master, first, second, out, grad,
+                 master, first, second, out, grad_out,
                  hs, cs, zs1, zsb, zs2, zr1, zrb, zr2, zhold, zown, zys, zyr,
-                 hraw, ho, co, ys1, ysb, ys2, yr1, yrb, yr2, yhold, yown, gbuf, adam,
-                 wsend, wbuf, asend, abuf, part, r1, rb, s2, r2, q, ug, kbuf, vbuf, qbuf, nbuf, att,
+                 hraw, ho, co, ys1, ysb, ys2, yr1, yrb, yr2, yhold, yown, gbuf, grad, adam,
+                 wsend, wbuf, asend, abuf, part, r1, q, ug, kbuf, vbuf, qbuf, nbuf, att,
                  loc_sem, send_sem, recv_sem):
     z, y_lo, core, x, y_hi = coords()
     y, mp, slot = y_hi * 2 + y_lo, x * 2 + y_hi, z * 2 + core
@@ -61,7 +60,7 @@
     z_up, z_down = place((z + 1) % 4, y_lo, core, x, y_hi), place((z + 3) % 4, y_lo, core, x, y_hi)
     y_place = [at_y((y + d) % 4) for d in range(1, 4)]
     x_place = [place(z, y_lo, core, (x + d) % 4, y_hi) for d in range(1, 4)]
-    axes = ((x, x_place[0], x_place[2]), (y, y_place[0], y_place[2]))
+    axes = ((x, x_place), (y, y_place))
     across = place(z, 1 - y_lo, core, x, y_hi)
     peers = [((x + i // 2) % 4, (y_hi + i % 2) % 2) for i in range(1, 8)]
     peer_place = [place(z, y_lo, core, px, py) for px, py in peers]
@@ -332,6 +331,10 @@
         for h in range(2):
             for copy in st["g", k, h]:
                 copy.wait_recv()
+        st["o", k] = []
+        for b in range(8):
+            cols = pl.ds(b * 512 + k * 128, 128)
+            st["o", k].append(local(grad.at[:, cols], grad_out.at[:, cols]))
         if k < 3:
             adam_fetch(k + 1)
         row = lax.broadcasted_iota(jnp.int32, (128, 120), 0)
@@ -399,34 +402,16 @@
             return carry
 
         lax.fori_loop(0, 4, body, 0)
-        lo, hi = pl.ds(0, 2), pl.ds(2, 2)
-        for d, (me, up, down) in enumerate(axes):
-            far, above, below = (me + 2) % 4, (me + 1) % 4, (me + 3) % 4
-            st["f1", k, d] = [send(part.at[k, d, far, lo], r1.at[k, d, 0], up),
-                              send(part.at[k, d, far, hi], r1.at[k, d, 1], down)]
-            st["fb", k, d] = [send(part.at[k, d, above, hi], rb.at[k, d, 0], up),
-                              send(part.at[k, d, below, lo], rb.at[k, d, 1], down)]
-
-    def f2(k):
-        for d, (me, up, down) in enumerate(axes):
-            above, below = (me + 1) % 4, (me + 3) % 4
-            st["f1", k, d][0].wait_recv()
-            s2[k, d, 0] = (part[k, d, above, pl.ds(0, 2)].astype(f32) + r1[k, d, 0].astype(f32)).astype(bf16)
-            first_half = send(s2.at[k, d, 0], r2.at[k, d, 0], up)
-            st["f1", k, d][1].wait_recv()
-            s2[k, d, 1] = (part[k, d, below, pl.ds(2, 2)].astype(f32) + r1[k, d, 1].astype(f32)).astype(bf16)
-            st["f2", k, d] = [first_half, send(s2.at[k, d, 1], r2.at[k, d, 1], down)]
+        for d, (me, devices) in enumerate(axes):
+            st["f1", k, d] = [send(part.at[k, d, (me + i) % 4], r1.at[k, d, i - 1], devices[i - 1]) for i in range(1, 4)]
 
     def f3(k):
-        for d, (me, up, down) in enumerate(axes):
-            st["fb", k, d][1].wait_recv()
-            st["f2", k, d][0].wait_recv()
-            q[k, d, pl.ds(0, 2)] = (part[k, d, me, pl.ds(0, 2)].astype(f32) + rb[k, d, 1].astype(f32)
-                                    + r2[k, d, 0].astype(f32)).astype(bf16)
-            st["fb", k, d][0].wait_recv()
-            st["f2", k, d][1].wait_recv()
-            q[k, d, pl.ds(2, 2)] = (part[k, d, me, pl.ds(2, 2)].astype(f32) + rb[k, d, 0].astype(f32)
-                                    + r2[k, d, 1].astype(f32)).astype(bf16)
+        for d, (me, _) in enumerate(axes):
+            total = part[k, d, me].astype(f32)
+            for i in range(3):
+                st["f1", k, d][i].wait_recv()
+                total = total + r1[k, d, i].astype(f32)
+            q[k, d] = total.astype(bf16)
             along, devices = (y, y_place) if d == 0 else (x, x_place)
             st["g", k, d] = [send(q.at[k, d, (along + i) % 4], ug.at[k, d, i - 1], devices[i - 1]) for i in range(1, 4)]
 
@@ -453,44 +438,48 @@
             copy.wait()
         if i < 5:
             cache_fetch(i + 1)
-        position = lax.broadcasted_iota(jnp.int32, (16, 128), 1)
-        when = lax.broadcasted_iota(jnp.int32, (16, 1), 0) // 4
-        heads = HEADS // KV_HEADS
-
-        def rows(n, carry):
-            for j in range(4):
-                r = i * 8 + n * 4 + j
-                qr = jnp.concatenate(
-                    [qbuf[t, g, pl.ds(r, 1), :] for t in range(4) for g in range(heads)], axis=0)
-                cached = lax.dot_general(qr.astype(bf16), kbuf[i % 2, n * 4 + j], (((1,), (1,)), ((), ())),
-                                         preferred_element_type=f32) * HEAD_DIM ** (-0.5)
-                cached = jnp.where(position < lengths[r], cached, -jnp.inf)
-                fresh = []
-                for s in range(4):
-                    score = jnp.sum(qr * nbuf[0, s, pl.ds(r, 1), :], axis=1, keepdims=True) * HEAD_DIM ** (-0.5)
-                    fresh.append(jnp.where(when >= s, score, -jnp.inf))
-                highest = jnp.max(cached, axis=1, keepdims=True)
-                for score in fresh:
-                    highest = jnp.maximum(highest, score)
-                cached = jnp.exp(cached - highest)
-                fresh = [jnp.exp(score - highest) for score in fresh]
-                total = jnp.sum(cached, axis=1, keepdims=True) + (fresh[0] + fresh[1]) + (fresh[2] + fresh[3])
-                result = jnp.dot((cached / total).astype(bf16), vbuf[i % 2, n * 4 + j], preferred_element_type=f32)
-                for s in range(4):
-                    weight = (fresh[s] / total).astype(bf16).astype(f32)
-                    result = result + weight * nbuf[1, s, pl.ds(r, 1), :]
-                for t in range(4):
-                    for g in range(heads):
-                        att[t, g, pl.ds(r, 1), :] = result[t * heads + g:t * heads + g + 1]
-            return carry
-
-        lax.fori_loop(0, 2, rows, 0)
+        lines = slice(i * 8, (i + 1) * 8)
+        lane = lax.broadcasted_iota(jnp.int32, (128, 128), 1)
+        line = lax.broadcasted_iota(jnp.int32, (128, 128), 0) % 8
+        when = lax.broadcasted_iota(jnp.int32, (128, 1), 0) // 32
+        asked = qbuf[:, :, lines, :].reshape(128, 128)
+        asked_low = asked.astype(bf16)
+        cached = jnp.zeros((128, 128), f32)
+        limit = jnp.zeros((128, 128), jnp.int32)
+        for j in range(8):
+            scores = lax.dot_general(asked_low, kbuf[i % 2, j], (((1,), (1,)), ((), ())), preferred_element_type=f32)
+            cached = jnp.where(line == j, scores, cached)
+            limit = jnp.where(line == j, lengths[i * 8 + j], limit)
+        cached = jnp.where(lane < limit, cached * HEAD_DIM ** (-0.5), -jnp.inf)
+        highest = jnp.max(cached, axis=1, keepdims=True)
+        fresh = []
+        for s in range(4):
+            product = asked.reshape(16, 8, 128) * nbuf[0, s, lines, :][None]
+            score = jnp.sum(product.reshape(128, 128), axis=1, keepdims=True) * HEAD_DIM ** (-0.5)
+            fresh.append(jnp.where(when >= s, score, -jnp.inf))
+            highest = jnp.maximum(highest, fresh[s])
+        cached = jnp.exp(cached - highest)
+        fresh = [jnp.exp(score - highest) for score in fresh]
+        total = jnp.sum(cached, axis=1, keepdims=True) + (fresh[0] + fresh[1]) + (fresh[2] + fresh[3])
+        weights = (cached / total).astype(bf16)
+        result = jnp.zeros((128, 128), f32)
+        for j in range(8):
+            sums = jnp.dot(weights, vbuf[i % 2, j], preferred_element_type=f32)
+            result = jnp.where(line == j, sums, result)
+        for s in range(4):
+            weight = (fresh[s] / total).astype(bf16).astype(f32)
+            value = jnp.broadcast_to(nbuf[1, s, lines, :][None], (16, 8, 128)).reshape(128, 128)
+            result = result + weight * value
+        att[:, :, lines, :] = result.reshape(4, 4, 8, 128)
 
     steps = {"za": za, "zb": zb_, "zc": zc, "zm": zm_, "ze": ze, "zf": zf_, "hf": hf, "bs": bs, "bf": bf, "ya": ya,
-             "yb": yb, "yc": yc, "ym": ym, "ye": ye, "ad": ad, "ga": ga, "gb": gb, "gc": gc, "mm": mm, "f2": f2,
+             "yb": yb, "yc": yc, "ym": ym, "ye": ye, "ad": ad, "ga": ga, "gb": gb, "gc": gc, "mm": mm,
              "f3": f3, "f5": f5, "ac": ac, "sw": sw, "ap": ap, "at": at}
     for name, *where in ORDER:
         steps[name](*where)
+    for k in range(4):
+        for copy in st["o", k]:
+            copy.wait()
     for copy in sends:
         copy.wait_send()
 
@@ -503,7 +492,7 @@
         return [pltpu.VMEM((n, 2, r, 128), bf16)] * 7 + [pltpu.VMEM((n, r, 256), f32)]
 
     copies = 12 + 16 + 1 + 8 * 11 + 4 * 33
-    locals_ = 4 + 16 + 12 + 4 * (24 + 1)
+    locals_ = 4 + 16 + 12 + 4 * (32 + 1)
     return pl.pallas_call(
         fused_kernel,
         out_shape=(jax.ShapeDtypeStruct((192, 512), bf16), jax.ShapeDtypeStruct((120, 4096), f32)),
@@ -511,7 +500,7 @@
         + [pl.BlockSpec(memory_space=pl.ANY)] * 2 + [pl.BlockSpec(memory_space=pltpu.VMEM)] * 2
         + [pl.BlockSpec(memory_space=pltpu.SMEM), pl.BlockSpec(memory_space=pltpu.VMEM)]
         + [pl.BlockSpec(memory_space=pl.ANY)] * 3,
-        out_specs=(pl.BlockSpec(memory_space=pltpu.VMEM),) * 2,
+        out_specs=(pl.BlockSpec(memory_space=pltpu.VMEM), pl.BlockSpec(memory_space=pl.ANY)),
         scratch_shapes=[
             pltpu.VMEM((8, 240, 1024), bf16),
             pltpu.VMEM((4, 2, 1024, 256), bf16),
@@ -523,13 +512,14 @@
             pltpu.VMEM((ny, 1024, 256), bf16),
             *ring(ny, 240),
             pltpu.VMEM((2, 2, 2, 2, 120, 128), f32),
+            pltpu.VMEM((120, 4096), f32),
             pltpu.VMEM((2, 3, 8, 120, 128), f32),
             pltpu.VMEM((4, 8, 16, 1024), bf16),
             pltpu.VMEM((4, 8, 8, 16, 1024), bf16),
             pltpu.VMEM((2, 192, 1024), bf16),
             pltpu.VMEM((2, 192, 1024), bf16),
             pltpu.VMEM((4, 2, 4, 4, 96, 128), bf16),
-            *[pltpu.VMEM((4, 2, 2, 2, 96, 128), bf16)] * 4,
+            pltpu.VMEM((4, 2, 3, 4, 96, 128), bf16),
             pltpu.VMEM((4, 2, 4, 96, 128), bf16),
             pltpu.VMEM((4, 2, 3, 96, 128), bf16),
             pltpu.VMEM((2, 8, 128, 128), bf16),

time: 125 us -> 122 us (0.976)
  Pallas kernels: 118 us -> 116 us
    pallas_call x1, Pallas kernels: 118 us -> 116 us  [fused(): pl.pallas_call(fused_kernel, out_shape=(jax.ShapeDtypeStruct((192, 512),...]
where the time goes in v7:
time: 122 us
  Pallas kernels  116 us (95%)
  other arithmetic  5.25 us (4%)
    pallas_call x1, Pallas kernels, fused(): pl.pallas_call(fused_kernel, out_shape=(jax.ShapeDtypeStruct((192, 512),...  116 us
    sub x1, other arithmetic, local(): master - learn_rate * (first_hat / (jnp.sqrt(second_hat) + adam_eps) + de...  5.25 us

profile of v7, /device:TPU:0, one launch (start us, length us, event | category | flops | bytes accessed | tf_op | source)
XLA Modules:
  0.0 122.3 jit_solution(17703519627072259662)
XLA Ops:
  0.6 0.0 copy-start
  0.6 0.0 copy-start.1
  0.7 0.0 copy-start.2
  0.7 115.7 %fused.1 = (bf16[192,512]{1,0:T(8,128)(2,1)}, f32[120,4096]{1,0:T(8,128)}) custom-call(bf16[512,1920]{1,0:T(8,128)(2,1)} %hidden_in.1, bf16[512,4096]{1,0:T(8,128)(2,1)} %cot.1, bf16[192,1920]{1,0:T(8,128)(2,1)} %bitcast.4, bf16[4,48,512]{2,1,0:T(8,128)(2,1)} %queries.1, bf16[48,128,128]{2,1,0:T(8,128)(2,1)} %keys.1, bf16[48,128,128]{2,1,0:T(8,128)(2,1)} %values.1, ...), custom_call_target="tpu_custom_call" | custom-call | flops 11274289152 | bytes 20971520 | tf_op jit(solution)/shard_map/fused/pallas_call | solution.py:496
  116.3 0.0 copy-done
  116.3 0.0 copy-done.1
  116.4 0.0 copy-done.2
  116.4 0.0 copy-start.3
  116.4 5.3 %multiply_subtract_fusion = (f32[120,4096]{1,0:T(8,128)}, f32[120,4096]{1,0:T(8,128)}, f32[120,4096]{1,0:T(8,128)}) fusion(f32[120,4096]{1,0:T(8,128)S(1)} %copy-done, f32[120,4096]{1,0:T(8,128)} %get-tuple-element.7, f32[120,4096]{1,0:T(8,128)S(1)} %copy-done.1, f32[120,4096]{1,0:T(8,128)S(1)} %copy-done.2), kind=kLoop, calls=%fused_computation.2 | loop fusion | flops 7372800 | bytes 13762560 | tf_op jit(solution)/shard_map/sub | solution.py:564
  121.6 0.0 copy-done.3
  121.6 0.7 copy.18
Async XLA Ops:
  0.6 115.7 %copy-start = (f32[120,4096]{1,0:T(8,128)S(1)}, f32[120,4096]{1,0:T(8,128)}, u32[]{:S(2)}) copy-start(f32[120,4096]{1,0:T(8,128)} %master.1) | copy-start | bytes 5898244
  0.6 115.7 %copy-start.1 = (f32[120,4096]{1,0:T(8,128)S(1)}, f32[120,4096]{1,0:T(8,128)}, u32[]{:S(2)}) copy-start(f32[120,4096]{1,0:T(8,128)} %first.1) | copy-start | bytes 5898244
  0.7 115.7 %copy-start.2 = (f32[120,4096]{1,0:T(8,128)S(1)}, f32[120,4096]{1,0:T(8,128)}, u32[]{:S(2)}) copy-start(f32[120,4096]{1,0:T(8,128)} %second.1) | copy-start | bytes 5898244
  116.4 5.3 %copy-start.3 = (bf16[192,512]{1,0:T(8,128)(2,1)S(1)}, bf16[192,512]{1,0:T(8,128)(2,1)}, u32[]{:S(2)}) copy-start(bf16[192,512]{1,0:T(8,128)(2,1)} %get-tuple-element.6) | copy-start | bytes 589828
